TPU v7x, 256 devices: a whole 4x4x8 slice. The times are simulated.
256 devices in a mesh: section: 32 (over y, x, z_lo), tensor: 8 (over z_hi, core).
Axes of the slice: x: 4, y: 4, z: 8 (z_hi: 4, z_lo: 2; z = z_hi * 2 + z_lo), core: 2. Of those that a mesh axis runs over, the one named last changes fastest.
Arguments:
- stashed_qk: bfloat16 [32, 2, 512, 6144], P('section', None, None, 'tensor'), may hold values from -24 to 24
- grad_heads: bfloat16 [32, 512, 6144], P('section', None, 'tensor'), may hold values from -6 to 6
- segment_ids: int32 [32, 512], replicated, may hold values from 0 to 3, never falling along the last dimension, each value on 1 to 256 neighbouring positions
- w_value: bfloat16 [32, 6144, 6144], P('section', None, 'tensor'), may hold values from -0.078125 to 0.078125
- grad_in: bfloat16 [32, 512, 6144], P('section', 'tensor'), may hold values from -4 to 4
Outputs:
- upstream: bfloat16 [32, 512, 6144], P('section', 'tensor')
All inputs are finite; a program needn't handle non-finite values.
Results may differ from a plain program's by a relative error of at most 0.02.
Values may be sent and summed in bfloat16 or wider, within the bound.
No kernel may reach another device: no remote copies, remote signals or barrier semaphores. Data moves between devices by JAX's collectives and lax.ppermute only.
A program may use at most 64 MiB of HBM per device.

v0:
```python
import jax
import jax.numpy as jnp
from jax import lax
from jax.sharding import PartitionSpec as P

HD = 128


def from_partner(block, axis, apart):
    count = lax.axis_size(axis)
    route = []
    for low in range(count):
        high = low | 1 << apart
        if high != low and high < count:
            route += [(low, high), (high, low)]
    return lax.ppermute(block, axis, route)


def passed_along(value, axis, by):
    peers = lax.axis_size(axis)
    pairs = [(i, i + by) for i in range(peers) if 0 <= i + by < peers]
    return lax.ppermute(value, axis, pairs)


def value_gradient(queries, key_rows, grad_heads, segment_row):
    row_count = queries.shape[0]
    head_count = queries.shape[1] // HD
    query_heads = queries.reshape(row_count, head_count, HD)
    key_heads = key_rows.reshape(row_count, head_count, HD)
    grad_split = grad_heads.reshape(row_count, head_count, HD)
    scores = jnp.einsum(
        "qhd,khd->hqk", query_heads, key_heads, preferred_element_type=jnp.float32
    ) * HD ** (-0.5)
    positions = jnp.arange(row_count, dtype=jnp.int32)
    visible = (positions[None, :] <= positions[:, None]) & (
        segment_row[None, :] == segment_row[:, None]
    )
    scores = jnp.where(visible[None], scores, -1e30)
    largest = jnp.max(scores, axis=2, keepdims=True)
    raised = jnp.exp(scores - largest)
    softmax_out = (raised / jnp.sum(raised, axis=2, keepdims=True)).astype(jnp.bfloat16)
    value_grad = jnp.einsum(
        "hqk,qhd->khd", softmax_out, grad_split, preferred_element_type=jnp.float32
    )
    return value_grad.astype(jnp.bfloat16).reshape(row_count, head_count * HD)


def body(stashed_qk, grad_heads, segment_ids, w_value, grad_in):
    section_index = lax.axis_index("section")
    section_count = lax.axis_size("section")
    levels = section_count.bit_length() - 1
    stashed = stashed_qk[0]
    for bit_number in range(levels):
        stashed = from_partner(stashed, "section", bit_number)
    queries, key_rows = (stashed[0], stashed[1])
    segment_row = lax.dynamic_index_in_dim(segment_ids, section_index, 0, keepdims=False)
    value_grad = value_gradient(queries, key_rows, grad_heads[0], segment_row)
    weight = w_value[0]
    summed = lax.psum_scatter(
        lax.dot_general(
            value_grad, weight, (((1,), (1,)), ((), ())), preferred_element_type=jnp.float32
        ).astype(jnp.bfloat16),
        "tensor",
        scatter_dimension=0,
        tiled=True,
    )
    combined = (summed.astype(jnp.float32) + grad_in[0].astype(jnp.float32)).astype(jnp.bfloat16)
    moved = passed_along(combined, "section", -1)
    return moved[None]


def solution(mesh):
    in_specs = (
        P("section", None, None, "tensor"),
        P("section", None, "tensor"),
        P(),
        P("section", None, "tensor"),
        P("section", "tensor", None),
    )
    out_specs = P("section", "tensor", None)
    return jax.shard_map(body, mesh=mesh, in_specs=in_specs, out_specs=out_specs, check_vma=False)
```

profile of v0, /device:TPU:46, one launch (start us, length us, event | category | flops | bytes accessed | tf_op | source)
XLA Modules:
  0.0 315.9 jit_solution(17727985309907238988)
XLA Ops:
  6.5 0.0 copy-start
  6.5 0.0 reduce-scatter.2.cloned.1.call-start
  6.5 1.7 copy.8
  8.3 0.2 collective-permute-start
  8.5 36.0 %collective-permute-done = bf16[2,512,768]{1,2,0:T(8,128)(2,1)S(1)} collective-permute-done((bf16[2,512,768]{1,2,0:T(8,128)(2,1)S(1)}, bf16[2,512,768]{1,2,0:T(8,128)(2,1)S(1)}, u32[]{:S(2)}, u32[]{:S(2)}) %collective-permute-start) | collective-permute-done | bytes 1572896 | tf_op jit(solution)/shard_map/ppermute | solution.py:16
  44.5 0.8 collective-permute-start.1
  45.3 34.4 %collective-permute-done.1 = bf16[2,512,768]{1,2,0:T(8,128)(2,1)S(1)} collective-permute-done((bf16[2,512,768]{1,2,0:T(8,128)(2,1)S(1)}, bf16[2,512,768]{1,2,0:T(8,128)(2,1)S(1)}, u32[]{:S(2)}, u32[]{:S(2)}) %collective-permute-start.1) | collective-permute-done | bytes 1572896 | tf_op jit(solution)/shard_map/ppermute | solution.py:16
  79.8 1.4 collective-permute-start.2
  81.2 34.4 %collective-permute-done.2 = bf16[2,512,768]{1,2,0:T(8,128)(2,1)S(1)} collective-permute-done((bf16[2,512,768]{1,2,0:T(8,128)(2,1)S(1)}, bf16[2,512,768]{1,2,0:T(8,128)(2,1)S(1)}, u32[]{:S(2)}, u32[]{:S(2)}) %collective-permute-start.2) | collective-permute-done | bytes 1572896 | tf_op jit(solution)/shard_map/ppermute | solution.py:16
  115.6 0.4 collective-permute-start.3
  116.1 33.1 %collective-permute-done.3 = bf16[2,512,768]{1,2,0:T(8,128)(2,1)} collective-permute-done((bf16[2,512,768]{1,2,0:T(8,128)(2,1)S(1)}, bf16[2,512,768]{1,2,0:T(8,128)(2,1)}, u32[]{:S(2)}, u32[]{:S(2)}) %collective-permute-start.3) | collective-permute-done | bytes 1572896 | tf_op jit(solution)/shard_map/ppermute | solution.py:16
  149.1 4.1 %collective-permute-start.4 = (bf16[2,512,768]{1,2,0:T(8,128)(2,1)}, bf16[2,512,768]{1,2,0:T(8,128)(2,1)S(1)}, u32[]{:S(2)}, u32[]{:S(2)}) collective-permute-start(bf16[2,512,768]{1,2,0:T(8,128)(2,1)} %collective-permute-done.3), channel_id=1, source_target_pairs={{0,128},{128,0},{8,136},{136,8},{16,144},{144,16},{24,152},{152,24... | collective-permute-start | bytes 4718600 | tf_op jit(solution)/shard_map/ppermute | solution.py:16
  153.2 1.4 copy.11
  154.6 0.0 copy-done
  154.7 0.2 fusion.13
  154.9 28.9 %collective-permute-done.4 = bf16[2,512,768]{1,2,0:T(8,128)(2,1)S(1)} collective-permute-done((bf16[2,512,768]{1,2,0:T(8,128)(2,1)}, bf16[2,512,768]{1,2,0:T(8,128)(2,1)S(1)}, u32[]{:S(2)}, u32[]{:S(2)}) %collective-permute-start.4) | collective-permute-done | bytes 1572896 | tf_op jit(solution)/shard_map/ppermute | solution.py:16
  183.8 1.0 fusion.18
  184.7 6.2 %fusion.19 = (f32[6,512]{1,0:T(8,128)S(1)}, f32[6,512,512]{1,2,0:T(8,128)}) fusion(pred[512,512]{0,1:T(8,128)(4,1)S(1)} %fusion.13, bf16[512,6,128]{0,2,1:T(8,128)(2,1)} %bitcast.27, bf16[512,6,128]{0,2,1:T(8,128)(2,1)S(1)} %bitcast.26), kind=kOutput, calls=%fused_computation.22 | convolution fusion | flops 408945152 | bytes 8138752 | tf_op jit(solution)/shard_map/sub | solution.py:40
  191.0 3.9 %fusion.12 = bf16[6,512,128]{1,2,0:T(8,128)(2,1)S(1)} fusion(bf16[512,6,128]{0,2,1:T(8,128)(2,1)S(1)} %bitcast.24, f32[6,512,512]{1,2,0:T(8,128)} %get-tuple-element.8, f32[6,512]{1,0:T(8,128)S(1)} %get-tuple-element.7), kind=kOutput, calls=%fused_computation.14 | convolution fusion | flops 406192128 | bytes 7876608 | tf_op jit(solution)/shard_map/hqk,qhd->khd/dot_general | solution.py:42
  194.9 10.7 %fusion.3 = bf16[512,6144]{1,0:T(8,128)(2,1)} fusion(bf16[512,768]{0,1:T(8,128)(2,1)S(1)} %bitcast.29, bf16[1,6144,768]{2,1,0:T(8,128)(2,1)} %param.8), kind=kOutput, calls=%fused_computation.3 | convolution fusion | flops 4834983936 | bytes 16515072 | tf_op jit(solution)/shard_map/dot_general | solution.py:60
  205.7 0.0 copy-start.1
  205.7 0.0 reduce-scatter.2.cloned.1.call-update
  205.7 79.3 %reduce-scatter.2.cloned.1.call-done = bf16[64,6144]{1,0:T(8,128)(2,1)} async-done(((bf16[512,6144]{1,0:T(8,128)(2,1)}), bf16[64,6144]{1,0:T(8,128)(2,1)}) %reduce-scatter.2.cloned.1.call-update) | async-done | bytes 786448 | tf_op jit(solution)/shard_map/reduce_scatter | solution.py:59
  285.0 0.0 copy-done.1
  285.0 1.3 fusion.11
  286.3 5.8 %collective-permute-start.5 = (bf16[64,6144]{1,0:T(8,128)(2,1)S(1)}, bf16[64,6144]{1,0:T(8,128)(2,1)S(1)}, u32[]{:S(2)}, u32[]{:S(2)}) collective-permute-start(bf16[64,6144]{1,0:T(8,128)(2,1)S(1)} %fusion.11), channel_id=1, source_target_pairs={{8,0},{16,8},{24,16},{32,24},{40,32},{48,40},{56,48},{64,56},{72,6... | collective-permute-start | bytes 2359304 | tf_op jit(solution)/shard_map/ppermute | solution.py:22
  292.1 16.1 %collective-permute-done.5 = bf16[64,6144]{1,0:T(8,128)(2,1)S(1)} collective-permute-done((bf16[64,6144]{1,0:T(8,128)(2,1)S(1)}, bf16[64,6144]{1,0:T(8,128)(2,1)S(1)}, u32[]{:S(2)}, u32[]{:S(2)}) %collective-permute-start.5) | collective-permute-done | bytes 786464 | tf_op jit(solution)/shard_map/ppermute | solution.py:22
  308.2 0.9 copy.17
  (1 shorter events, 0.0 us)
Async XLA Ops:
  6.5 148.1 %copy-start = (s32[32,512]{1,0:T(8,128)S(1)}, s32[32,512]{1,0:T(8,128)}, u32[]{:S(2)}) copy-start(s32[32,512]{1,0:T(8,128)} %param.7) | copy-start | bytes 196612
  6.5 278.5 %reduce-scatter.2.cloned.1.call-start = ((), (), s32[]{:S(2)}) async-start(), calls=%async_computation.1 | async-start | bytes 7077888 | tf_op jit(solution)/shard_map/reduce_scatter | solution.py:59
  8.3 36.2 %collective-permute-start = (bf16[2,512,768]{1,2,0:T(8,128)(2,1)S(1)}, bf16[2,512,768]{1,2,0:T(8,128)(2,1)S(1)}, u32[]{:S(2)}, u32[]{:S(2)}) collective-permute-start(bf16[2,512,768]{1,2,0:T(8,128)(2,1)S(1)} %bitcast.23), channel_id=1, source_target_pairs={{0,8},{8,0},{16,24},{24,16},{32,40},{40,32},{48,56},{56,48},{64,72... | collective-permute-start | bytes 4718600 | tf_op jit(solution)/shard_map/ppermute | solution.py:16
  44.5 35.3 %collective-permute-start.1 = (bf16[2,512,768]{1,2,0:T(8,128)(2,1)S(1)}, bf16[2,512,768]{1,2,0:T(8,128)(2,1)S(1)}, u32[]{:S(2)}, u32[]{:S(2)}) collective-permute-start(bf16[2,512,768]{1,2,0:T(8,128)(2,1)S(1)} %collective-permute-done), channel_id=1, source_target_pairs={{0,16},{16,0},{8,24},{24,8},{32,48},{48,32},{40,56},{56,40},{64,80... | collective-permute-start | bytes 4718600 | tf_op jit(solution)/shard_map/ppermute | solution.py:16
  79.8 35.8 %collective-permute-start.2 = (bf16[2,512,768]{1,2,0:T(8,128)(2,1)S(1)}, bf16[2,512,768]{1,2,0:T(8,128)(2,1)S(1)}, u32[]{:S(2)}, u32[]{:S(2)}) collective-permute-start(bf16[2,512,768]{1,2,0:T(8,128)(2,1)S(1)} %collective-permute-done.1), channel_id=1, source_target_pairs={{0,32},{32,0},{8,40},{40,8},{16,48},{48,16},{24,56},{56,24},{64,96... | collective-permute-start | bytes 4718600 | tf_op jit(solution)/shard_map/ppermute | solution.py:16
  115.6 33.5 %collective-permute-start.3 = (bf16[2,512,768]{1,2,0:T(8,128)(2,1)S(1)}, bf16[2,512,768]{1,2,0:T(8,128)(2,1)}, u32[]{:S(2)}, u32[]{:S(2)}) collective-permute-start(bf16[2,512,768]{1,2,0:T(8,128)(2,1)S(1)} %collective-permute-done.2), channel_id=1, source_target_pairs={{0,64},{64,0},{8,72},{72,8},{16,80},{80,16},{24,88},{88,24},{32,96... | collective-permute-start | bytes 4718600 | tf_op jit(solution)/shard_map/ppermute | solution.py:16
  149.1 34.6 %collective-permute-start.4 = (bf16[2,512,768]{1,2,0:T(8,128)(2,1)}, bf16[2,512,768]{1,2,0:T(8,128)(2,1)S(1)}, u32[]{:S(2)}, u32[]{:S(2)}) collective-permute-start(bf16[2,512,768]{1,2,0:T(8,128)(2,1)} %collective-permute-done.3), channel_id=1, source_target_pairs={{0,128},{128,0},{8,136},{136,8},{16,144},{144,16},{24,152},{152,24... | collective-permute-start | bytes 4718600 | tf_op jit(solution)/shard_map/ppermute | solution.py:16
  205.7 79.4 %copy-start.1 = (bf16[1,64,6144]{2,1,0:T(8,128)(2,1)S(1)}, bf16[1,64,6144]{2,1,0:T(8,128)(2,1)}, u32[]{:S(2)}) copy-start(bf16[1,64,6144]{2,1,0:T(8,128)(2,1)} %param.9) | copy-start | bytes 2359300
  286.3 21.8 %collective-permute-start.5 = (bf16[64,6144]{1,0:T(8,128)(2,1)S(1)}, bf16[64,6144]{1,0:T(8,128)(2,1)S(1)}, u32[]{:S(2)}, u32[]{:S(2)}) collective-permute-start(bf16[64,6144]{1,0:T(8,128)(2,1)S(1)} %fusion.11), channel_id=1, source_target_pairs={{8,0},{16,8},{24,16},{32,24},{40,32},{48,40},{56,48},{64,56},{72,6... | collective-permute-start | bytes 2359304 | tf_op jit(solution)/shard_map/ppermute | solution.py:22
Sparse Core Ops, SparseCore 0:
  205.8 79.1 reduce-scatter.1
where the time goes:
time: 317 us; the launch traced here: 316 us
  waiting for transfers between devices  262 us (83%)
  matrix products  20.9 us (7%)
  between operations  13.4 us (4%)
  starting transfers between devices  12.7 us (4%)
  local copies, waits for them, and re-layouts  5.04 us (2%)
    ppermute x5, waiting for transfers between devices, from_partner(): return lax.ppermute(block, axis, route)  167 us
    reduce_scatter x1, waiting for transfers between devices, body(): lax.psum_scatter(lax.dot_general(value_grad, weight, (((1,), (1,)), ((),...  79.3 us
    ppermute x1, waiting for transfers between devices, passed_along(): return lax.ppermute(value, axis, pairs)  16.1 us
    dot_general x1, matrix products, body(): lax.dot_general(value_grad, weight, (((1,), (1,)), ((), ())), preferred_e...  10.7 us
    ppermute x5, starting transfers between devices, from_partner(): return lax.ppermute(block, axis, route)  6.95 us
  transfers between devices with their start and end apart: 7, of which 7 were waited for; matrix products, arithmetic and copies ran while one was open for 1% of the time, Pallas kernels for 0%

commit v1 on v0

v1 whole, which is shorter than its diff:
```python
import jax
import jax.numpy as jnp
from jax import lax
from jax.sharding import PartitionSpec as P

HD = 128
TOK = 512
FEAT = 6144
AXES = ("section", "tensor")
PIECES = 4


def place_of(device):
    section, tensor = divmod(device, 8)
    return section // 8, section // 2 % 4, tensor // 2 * 2 + section % 2, tensor % 2


def device_at(y, x, z, core):
    section = (y % 4) * 8 + (x % 4) * 2 + z % 2
    return section * 8 + z % 8 // 2 * 2 + core


def sent(value, target):
    pairs = []
    for device in range(256):
        place = target(*place_of(device))
        if place is not None:
            pairs.append((device, device_at(*place)))
    return lax.ppermute(value, AXES, pairs)


def mirror(y, x, z, core):
    return 3 - y, 3 - x, z ^ 1, core


def other_core(y, x, z, core):
    return y, x, z, 1 - core


def along_z(by):
    return lambda y, x, z, core: (y, x, z + by, core)


def previous(y, x, z, flip):
    if z % 2 == 0:
        return (y, x, z) if flip else None
    if x > 0:
        return y, x - 1, z
    return (y - 1, 3, z) if y > 0 else None


def to_previous(flip):
    def target(y, x, z, core):
        place = previous(y, x, z, flip)
        return None if place is None else place + (core ^ flip,)

    return target


def value_gradient(queries, key_rows, grad_heads, segment_row):
    row_count = queries.shape[0]
    head_count = queries.shape[1] // HD
    query_heads = queries.reshape(row_count, head_count, HD)
    key_heads = key_rows.reshape(row_count, head_count, HD)
    grad_split = grad_heads.reshape(row_count, head_count, HD)
    scores = jnp.einsum(
        "qhd,khd->hqk", query_heads, key_heads, preferred_element_type=jnp.float32
    ) * HD ** (-0.5)
    positions = jnp.arange(row_count, dtype=jnp.int32)
    visible = (positions[None, :] <= positions[:, None]) & (
        segment_row[None, :] == segment_row[:, None]
    )
    scores = jnp.where(visible[None], scores, -1e30)
    largest = jnp.max(scores, axis=2, keepdims=True)
    raised = jnp.exp(scores - largest)
    softmax_out = (raised / jnp.sum(raised, axis=2, keepdims=True)).astype(jnp.bfloat16)
    value_grad = jnp.einsum(
        "hqk,qhd->khd", softmax_out, grad_split, preferred_element_type=jnp.float32
    )
    return value_grad.astype(jnp.bfloat16).reshape(row_count, head_count * HD)


def body(stashed_qk, grad_heads, segment_ids, w_value, grad_in):
    section = lax.axis_index("section")
    tensor = lax.axis_index("tensor")
    z_low, z_high, core = section % 2, tensor // 2, tensor % 2
    half = FEAT // 2
    piece = half // PIECES

    stashed = sent(stashed_qk[0], mirror)

    weight = w_value[0]
    kept = lax.dynamic_slice_in_dim(weight, core * half, half, 0)
    given = lax.dynamic_slice_in_dim(weight, (1 - core) * half, half, 0)
    taken = sent(given, other_core)
    rows = grad_in[0]
    residual_kept = lax.dynamic_slice_in_dim(rows, core * half, half, 1)
    residual_taken = sent(lax.dynamic_slice_in_dim(rows, (1 - core) * half, half, 1), other_core)
    residual = jnp.where(
        core == 0,
        jnp.concatenate([residual_kept, residual_taken], 0),
        jnp.concatenate([residual_taken, residual_kept], 0),
    )

    segment_row = lax.dynamic_index_in_dim(segment_ids, section, 0, keepdims=False)
    own_grad = value_gradient(stashed[0], stashed[1], grad_heads[0], segment_row)
    other_grad = sent(own_grad, other_core)
    value_grad = jnp.concatenate([own_grad, other_grad], 1)
    base = (z_high + z_low) * 128 % TOK
    value_grad = lax.dynamic_slice_in_dim(
        jnp.concatenate([value_grad, value_grad], 0), base, TOK, 0
    )
    joined = jnp.concatenate([kept, taken], 1)

    def product(rows, columns):
        return lax.dot_general(
            rows, columns, (((1,), (1,)), ((), ())), preferred_element_type=jnp.float32
        )

    far = []
    for n in range(PIECES):
        columns = joined[n * piece : (n + 1) * piece]
        sums = product(value_grad[128:384], columns).astype(jnp.bfloat16)
        far.append((sent(sums[:128], along_z(2)), sent(sums[128:], along_z(-2))))
    near = []
    for n in range(PIECES):
        columns = joined[n * piece : (n + 1) * piece]
        added = residual[:, n * piece : (n + 1) * piece].astype(jnp.float32)
        up = product(value_grad[:128], columns) + far[n][0].astype(jnp.float32)
        down = product(value_grad[384:], columns) + far[n][1].astype(jnp.float32)
        up = up + jnp.where(z_low == 0, added, 0.0)
        down = down + jnp.where(z_low == 1, added, 0.0)
        near.append(
            (
                sent(up.astype(jnp.bfloat16), along_z(1)),
                sent(down.astype(jnp.bfloat16), along_z(-1)),
            )
        )
    straight, crossed = [], []
    for n in range(PIECES):
        total = (near[n][0].astype(jnp.float32) + near[n][1].astype(jnp.float32)).astype(jnp.bfloat16)
        same = lax.dynamic_slice_in_dim(total, core * 64, 64, 0)
        cross = lax.dynamic_slice_in_dim(total, (1 - core) * 64, 64, 0)
        straight.append(jnp.where(z_low == 0, same, sent(same, to_previous(0))))
        crossed.append(sent(cross, to_previous(1)))
    straight = jnp.concatenate(straight, 1)
    crossed = jnp.concatenate(crossed, 1)
    return jnp.where(
        core == 0,
        jnp.concatenate([straight, crossed], 1),
        jnp.concatenate([crossed, straight], 1),
    )[None]


def solution(mesh):
    in_specs = (
        P("section", None, None, "tensor"),
        P("section", None, "tensor"),
        P(),
        P("section", None, "tensor"),
        P("section", "tensor", None),
    )
    out_specs = P("section", "tensor", None)
    return jax.shard_map(body, mesh=mesh, in_specs=in_specs, out_specs=out_specs, check_vma=False)
```

time: 317 us -> 157 us (0.50)
  waiting for transfers between devices: 262 us -> 52.2 us
  starting transfers between devices: 12.7 us -> 58.7 us
  between operations: 13.4 us -> 0.57 us
  other arithmetic: 1.52 us -> 11.7 us
  local copies, waits for them, and re-layouts: 5.04 us -> 12.4 us
    ppermute x6 -> x28, waiting for transfers between devices: 183 us -> 52.2 us  [sent(): return lax.ppermute(value, AXES, pairs)]
    reduce_scatter x1 -> x0, waiting for transfers between devices: 79.3 us -> none  [body(): lax.psum_scatter(lax.dot_general(value_grad, weight, (((1,), (1,)), ((),...]
    ppermute x6 -> x28, starting transfers between devices: 12.7 us -> 58.7 us  [sent(): return lax.ppermute(value, AXES, pairs)]
    concatenate x0 -> x3, other arithmetic: none -> 10.1 us  [the longest x1 5.98 us: body(): jnp.concatenate([value_grad, value_grad], 0)]
    dynamic_slice x1 -> x7, local copies, waits for them, and re-layouts: 0.01 us -> 8.19 us  [the longest x1 8.03 us: body(): given = lax.dynamic_slice_in_dim(weight, (1 - core) * half, half, 0)]
    dot_general x1 -> x12, matrix products: 10.7 us -> 10.6 us  [product(): lax.dot_general(rows, columns, (((1,), (1,)), ((), ())), preferred_elemen...]
  transfers between devices with their start and end apart: 7 -> 28, of which waited for: 7 -> 11; matrix products, arithmetic and copies ran while one was open for 1% -> 20% of each run, Pallas kernels for 0% -> 0%
where the time goes in v1:
time: 157 us
  starting transfers between devices  58.7 us (37%)
  waiting for transfers between devices  52.2 us (33%)
  matrix products  20.9 us (13%)
  local copies, waits for them, and re-layouts  12.4 us (8%)
  other arithmetic  11.7 us (7%)
    ppermute x28, starting transfers between devices, sent(): return lax.ppermute(value, AXES, pairs)  58.7 us
    ppermute x28, waiting for transfers between devices, sent(): return lax.ppermute(value, AXES, pairs)  52.2 us
    dot_general x12, matrix products, product(): lax.dot_general(rows, columns, (((1,), (1,)), ((), ())), preferred_elemen...  10.6 us
    dynamic_slice x1, local copies, waits for them, and re-layouts, body(): given = lax.dynamic_slice_in_dim(weight, (1 - core) * half, half, 0)  8.03 us
    sub x1, matrix products, value_gradient(): raised = jnp.exp(scores - largest)  6.3 us
    concatenate x1, other arithmetic, body(): jnp.concatenate([value_grad, value_grad], 0)  5.98 us
    concatenate x1, other arithmetic, body(): joined = jnp.concatenate([kept, taken], 1)  4.1 us
    dot_general x1, matrix products, value_gradient(): jnp.einsum('hqk,qhd->khd', softmax_out, grad_split, preferred_element_typ...  4.01 us
  transfers between devices with their start and end apart: 28, of which 11 were waited for; matrix products, arithmetic and copies ran while one was open for 20% of the time, Pallas kernels for 0%

profile of v1, /device:TPU:46, one launch (start us, length us, event | category | flops | bytes accessed | tf_op | source)
XLA Modules:
  0.0 156.5 jit_solution(16915086366065092534)
XLA Ops:
  0.0 8.0 %dynamic-slice_bitcast_fusion = (bf16[3072,768]{1,0:T(8,128)(2,1)}, bf16[3072,768]{1,0:T(8,128)(2,1)}) fusion(bf16[1,6144,768]{2,1,0:T(8,128)(2,1)} %param.8, s32[]{:T(128)S(6)} %select_n.141, s32[]{:T(128)S(6)} %select_n.140), kind=kLoop, calls=%fused_computation.11 | loop fusion | bytes 18874376 | tf_op jit(solution)/shard_map/dynamic_slice | solution.py:94
  8.7 1.1 collective-permute-start
  9.9 2.3 %copy.11 = bf16[1,512,768]{1,2,0:T(8,128)(2,1)} copy(bf16[1,512,768]{2,1,0:T(8,128)(2,1)} %param.6) | data formatting | bytes 1572864 | tf_op args[1]
  12.4 36.3 %collective-permute-done = bf16[2,512,768]{1,2,0:T(8,128)(2,1)S(1)} collective-permute-done((bf16[2,512,768]{1,2,0:T(8,128)(2,1)S(1)}, bf16[2,512,768]{1,2,0:T(8,128)(2,1)S(1)}, u32[]{:S(2)}, u32[]{:S(2)}) %collective-permute-start) | collective-permute-done | bytes 1572896 | tf_op jit(solution)/shard_map/ppermute | solution.py:29
  49.6 6.3 %fusion.51 = (f32[6,512]{1,0:T(8,128)S(1)}, f32[6,512,512]{1,2,0:T(8,128)}) fusion(pred[512,512]{0,1:T(8,128)(4,1)S(1)} %fusion.29, bf16[512,6,128]{0,2,1:T(8,128)(2,1)} %bitcast.60, bf16[512,6,128]{0,2,1:T(8,128)(2,1)S(1)} %bitcast.59), kind=kOutput, calls=%fused_computation.124 | convolution fusion | flops 408945152 | bytes 8138752 | tf_op jit(solution)/shard_map/sub | solution.py:75
  55.9 4.0 %fusion.12 = bf16[6,512,128]{1,2,0:T(8,128)(2,1)S(1)} fusion(bf16[512,6,128]{0,2,1:T(8,128)(2,1)S(1)} %bitcast.58, f32[6,512,512]{1,2,0:T(8,128)} %get-tuple-element.40, f32[6,512]{1,0:T(8,128)S(1)} %get-tuple-element.39), kind=kOutput, calls=%fused_computation.28 | convolution fusion | flops 406192128 | bytes 7876608 | tf_op jit(solution)/shard_map/hqk,qhd->khd/dot_general | solution.py:77
  60.9 2.0 %collective-permute-done.4 = bf16[64,3072]{1,0:T(8,128)(2,1)S(1)} collective-permute-done((bf16[64,3072]{1,0:T(8,128)(2,1)S(1)}, bf16[64,3072]{1,0:T(8,128)(2,1)S(1)}, u32[]{:S(2)}, u32[]{:S(2)}) %collective-permute-start.4) | collective-permute-done | bytes 393248 | tf_op jit(solution)/shard_map/ppermute | solution.py:29
  63.1 6.0 %fusion.10 = bf16[512,1536]{0,1:T(8,128)(2,1)S(1)} fusion(s32[]{:T(128)S(6)} %select_n.139, bf16[512,768]{0,1:T(8,128)(2,1)S(1)} %bitcast.62, bf16[512,768]{0,1:T(8,128)(2,1)S(1)} %collective-permute-done.1), kind=kLoop, calls=%fused_computation.26 | loop fusion | flops 6291456 | bytes 3145732 | tf_op jit(solution)/shard_map/concatenate | solution.py:111
  69.1 4.1 %pad_maximum_fusion = (bf16[768,1536]{1,0:T(8,128)(2,1)S(1)}, bf16[768,1536]{1,0:T(8,128)(2,1)S(1)}, bf16[768,1536]{1,0:T(8,128)(2,1)S(1)}, bf16[768,1536]{1,0:T(8,128)(2,1)S(1)}) fusion(bf16[3072,768]{1,0:T(8,128)(2,1)} %collective-permute-done.2, bf16[3072,768]{1,0:T(8,128)(2,1)} %get-tuple-element.10), kind=kLoop, calls=%fused_computation.24 | loop fusion | flops 18874368 | bytes 18874368 | tf_op jit(solution)/shard_map/concatenate | solution.py:113
  74.0 5.5 %collective-permute-start.6 = (bf16[128,768]{1,0:T(8,128)(2,1)S(1)}, bf16[128,768]{1,0:T(8,128)(2,1)S(1)}, u32[]{:S(2)}, u32[]{:S(2)}) collective-permute-start(bf16[128,768]{1,0:T(8,128)(2,1)S(1)} %get-tuple-element.22), channel_id=1, source_target_pairs={{0,6},{1,7},{2,0},{3,1},{4,2},{5,3},{6,4},{7,5},{8,14},{9,15},{10,... | collective-permute-start | bytes 589832 | tf_op jit(solution)/shard_map/ppermute | solution.py:29
  80.4 4.2 %collective-permute-start.11 = (bf16[128,768]{1,0:T(8,128)(2,1)S(1)}, bf16[128,768]{1,0:T(8,128)(2,1)S(1)}, u32[]{:S(2)}, u32[]{:S(2)}) collective-permute-start(bf16[128,768]{1,0:T(8,128)(2,1)S(1)} %get-tuple-element.20), channel_id=1, source_target_pairs={{0,6},{1,7},{2,0},{3,1},{4,2},{5,3},{6,4},{7,5},{8,14},{9,15},{10,... | collective-permute-start | bytes 589832 | tf_op jit(solution)/shard_map/ppermute | solution.py:29
  85.5 4.2 %collective-permute-start.16 = (bf16[128,768]{1,0:T(8,128)(2,1)S(1)}, bf16[128,768]{1,0:T(8,128)(2,1)S(1)}, u32[]{:S(2)}, u32[]{:S(2)}) collective-permute-start(bf16[128,768]{1,0:T(8,128)(2,1)S(1)} %get-tuple-element.18), channel_id=1, source_target_pairs={{0,6},{1,7},{2,0},{3,1},{4,2},{5,3},{6,4},{7,5},{8,14},{9,15},{10,... | collective-permute-start | bytes 589832 | tf_op jit(solution)/shard_map/ppermute | solution.py:29
  91.6 1.7 %collective-permute-done.11 = bf16[128,768]{1,0:T(8,128)(2,1)S(1)} collective-permute-done((bf16[128,768]{1,0:T(8,128)(2,1)S(1)}, bf16[128,768]{1,0:T(8,128)(2,1)S(1)}, u32[]{:S(2)}, u32[]{:S(2)}) %collective-permute-start.11) | collective-permute-done | bytes 196640 | tf_op jit(solution)/shard_map/ppermute | solution.py:29
  93.2 4.7 %collective-permute-start.21 = (bf16[128,768]{1,0:T(8,128)(2,1)S(1)}, bf16[128,768]{1,0:T(8,128)(2,1)S(1)}, u32[]{:S(2)}, u32[]{:S(2)}) collective-permute-start(bf16[128,768]{1,0:T(8,128)(2,1)S(1)} %get-tuple-element.16), channel_id=1, source_target_pairs={{0,6},{1,7},{2,0},{3,1},{4,2},{5,3},{6,4},{7,5},{8,14},{9,15},{10,... | collective-permute-start | bytes 589832 | tf_op jit(solution)/shard_map/ppermute | solution.py:29
  99.9 2.3 %collective-permute-done.9 = bf16[128,768]{1,0:T(8,128)(2,1)S(1)} collective-permute-done((bf16[128,768]{1,0:T(8,128)(2,1)S(1)}, bf16[128,768]{1,0:T(8,128)(2,1)S(1)}, u32[]{:S(2)}, u32[]{:S(2)}) %collective-permute-start.9) | collective-permute-done | bytes 196640 | tf_op jit(solution)/shard_map/ppermute | solution.py:29
  102.2 8.7 %collective-permute-start.7 = (bf16[128,768]{1,0:T(8,128)(2,1)S(1)}, bf16[128,768]{1,0:T(8,128)(2,1)S(1)}, u32[]{:S(2)}, u32[]{:S(2)}) collective-permute-start(bf16[128,768]{1,0:T(8,128)(2,1)S(1)} %fusion.27), channel_id=1, source_target_pairs={{0,14},{1,15},{2,8},{3,9},{4,10},{5,11},{6,12},{7,13},{8,0},{9,1},... | collective-permute-start | bytes 589832 | tf_op jit(solution)/shard_map/ppermute | solution.py:29
  111.8 1.2 collective-permute-start.5
  115.9 1.2 collective-permute-start.10
  118.0 1.9 %collective-permute-start.17 = (bf16[128,768]{1,0:T(8,128)(2,1)S(1)}, bf16[128,768]{1,0:T(8,128)(2,1)S(1)}, u32[]{:S(2)}, u32[]{:S(2)}) collective-permute-start(bf16[128,768]{1,0:T(8,128)(2,1)S(1)} %fusion.23), channel_id=1, source_target_pairs={{0,14},{1,15},{2,8},{3,9},{4,10},{5,11},{6,12},{7,13},{8,0},{9,1},... | collective-permute-start | bytes 589832 | tf_op jit(solution)/shard_map/ppermute | solution.py:29
  122.0 2.3 %collective-permute-start.22 = (bf16[128,768]{1,0:T(8,128)(2,1)S(1)}, bf16[128,768]{1,0:T(8,128)(2,1)S(1)}, u32[]{:S(2)}, u32[]{:S(2)}) collective-permute-start(bf16[128,768]{1,0:T(8,128)(2,1)S(1)} %fusion.21), channel_id=1, source_target_pairs={{0,14},{1,15},{2,8},{3,9},{4,10},{5,11},{6,12},{7,13},{8,0},{9,1},... | collective-permute-start | bytes 589832 | tf_op jit(solution)/shard_map/ppermute | solution.py:29
  124.4 1.8 %collective-permute-done.10 = bf16[128,768]{1,0:T(8,128)(2,1)S(1)} collective-permute-done((bf16[128,768]{1,0:T(8,128)(2,1)S(1)}, bf16[128,768]{1,0:T(8,128)(2,1)S(1)}, u32[]{:S(2)}, u32[]{:S(2)}) %collective-permute-start.10) | collective-permute-done | bytes 196640 | tf_op jit(solution)/shard_map/ppermute | solution.py:29
  126.2 1.9 %collective-permute-start.24 = (bf16[64,768]{1,0:T(8,128)(2,1)S(1)}, bf16[64,768]{1,0:T(8,128)(2,1)S(1)}, u32[]{:S(2)}, u32[]{:S(2)}) collective-permute-start(bf16[64,768]{1,0:T(8,128)(2,1)S(1)} %get-tuple-element.37), channel_id=1, source_target_pairs={{0,1},{1,0},{2,3},{3,2},{4,5},{5,4},{6,7},{7,6},{16,17},{17,16},{1... | collective-permute-start | bytes 294920 | tf_op jit(solution)/shard_map/ppermute | solution.py:29
  128.2 1.9 %collective-permute-start.25 = (bf16[64,768]{1,0:T(8,128)(2,1)S(1)}, bf16[64,768]{1,0:T(8,128)(2,1)S(1)}, u32[]{:S(2)}, u32[]{:S(2)}) collective-permute-start(bf16[64,768]{1,0:T(8,128)(2,1)S(1)} %get-tuple-element.35), channel_id=1, source_target_pairs={{0,1},{1,0},{2,3},{3,2},{4,5},{5,4},{6,7},{7,6},{16,17},{17,16},{1... | collective-permute-start | bytes 294920 | tf_op jit(solution)/shard_map/ppermute | solution.py:29
  130.5 1.9 %collective-permute-start.26 = (bf16[64,768]{1,0:T(8,128)(2,1)S(1)}, bf16[64,768]{1,0:T(8,128)(2,1)S(1)}, u32[]{:S(2)}, u32[]{:S(2)}) collective-permute-start(bf16[64,768]{1,0:T(8,128)(2,1)S(1)} %get-tuple-element.33), channel_id=1, source_target_pairs={{0,1},{1,0},{2,3},{3,2},{4,5},{5,4},{6,7},{7,6},{16,17},{17,16},{1... | collective-permute-start | bytes 294920 | tf_op jit(solution)/shard_map/ppermute | solution.py:29
  133.6 5.7 %collective-permute-start.27 = (bf16[64,768]{1,0:T(8,128)(2,1)S(1)}, bf16[64,768]{1,0:T(8,128)(2,1)S(1)}, u32[]{:S(2)}, u32[]{:S(2)}) collective-permute-start(bf16[64,768]{1,0:T(8,128)(2,1)S(1)} %get-tuple-element.31), channel_id=1, source_target_pairs={{0,1},{1,0},{2,3},{3,2},{4,5},{5,4},{6,7},{7,6},{16,17},{17,16},{1... | collective-permute-start | bytes 294920 | tf_op jit(solution)/shard_map/ppermute | solution.py:29
  139.4 1.9 %collective-permute-start.8 = (bf16[64,768]{1,0:T(8,128)(2,1)S(1)}, bf16[64,768]{1,0:T(8,128)(2,1)S(1)}, u32[]{:S(2)}, u32[]{:S(2)}) collective-permute-start(bf16[64,768]{1,0:T(8,128)(2,1)S(1)} %get-tuple-element.38), channel_id=1, source_target_pairs={{24,8},{25,9},{26,10},{27,11},{28,12},{29,13},{30,14},{31,15},{40,... | collective-permute-start | bytes 294920 | tf_op jit(solution)/shard_map/ppermute | solution.py:29
  141.3 2.5 %collective-permute-start.13 = (bf16[64,768]{1,0:T(8,128)(2,1)S(1)}, bf16[64,768]{1,0:T(8,128)(2,1)S(1)}, u32[]{:S(2)}, u32[]{:S(2)}) collective-permute-start(bf16[64,768]{1,0:T(8,128)(2,1)S(1)} %get-tuple-element.36), channel_id=1, source_target_pairs={{24,8},{25,9},{26,10},{27,11},{28,12},{29,13},{30,14},{31,15},{40,... | collective-permute-start | bytes 294920 | tf_op jit(solution)/shard_map/ppermute | solution.py:29
  143.8 3.0 %collective-permute-start.18 = (bf16[64,768]{1,0:T(8,128)(2,1)S(1)}, bf16[64,768]{1,0:T(8,128)(2,1)S(1)}, u32[]{:S(2)}, u32[]{:S(2)}) collective-permute-start(bf16[64,768]{1,0:T(8,128)(2,1)S(1)} %get-tuple-element.34), channel_id=1, source_target_pairs={{24,8},{25,9},{26,10},{27,11},{28,12},{29,13},{30,14},{31,15},{40,... | collective-permute-start | bytes 294920 | tf_op jit(solution)/shard_map/ppermute | solution.py:29
  146.8 2.2 %collective-permute-start.23 = (bf16[64,768]{1,0:T(8,128)(2,1)S(1)}, bf16[64,768]{1,0:T(8,128)(2,1)S(1)}, u32[]{:S(2)}, u32[]{:S(2)}) collective-permute-start(bf16[64,768]{1,0:T(8,128)(2,1)S(1)} %get-tuple-element.32), channel_id=1, source_target_pairs={{24,8},{25,9},{26,10},{27,11},{28,12},{29,13},{30,14},{31,15},{40,... | collective-permute-start | bytes 294920 | tf_op jit(solution)/shard_map/ppermute | solution.py:29
  149.1 1.2 collective-permute-done.13
  150.3 2.1 %collective-permute-done.18 = bf16[64,768]{1,0:T(8,128)(2,1)S(1)} collective-permute-done((bf16[64,768]{1,0:T(8,128)(2,1)S(1)}, bf16[64,768]{1,0:T(8,128)(2,1)S(1)}, u32[]{:S(2)}, u32[]{:S(2)}) %collective-permute-start.18) | collective-permute-done | bytes 98336 | tf_op jit(solution)/shard_map/ppermute | solution.py:29
  152.4 3.0 %collective-permute-done.23 = bf16[64,768]{1,0:T(8,128)(2,1)S(1)} collective-permute-done((bf16[64,768]{1,0:T(8,128)(2,1)S(1)}, bf16[64,768]{1,0:T(8,128)(2,1)S(1)}, u32[]{:S(2)}, u32[]{:S(2)}) %collective-permute-start.23) | collective-permute-done | bytes 98336 | tf_op jit(solution)/shard_map/ppermute | solution.py:29
  (81 shorter events, 18.9 us)
Async XLA Ops:
  0.0 12.2 %copy-start = (s32[32,512]{1,0:T(8,128)S(1)}, s32[32,512]{1,0:T(8,128)}, u32[]{:S(2)}) copy-start(s32[32,512]{1,0:T(8,128)} %param.7) | copy-start | bytes 196612
  0.0 8.0 %copy-start.1 = (bf16[1,2,512,768]{3,2,1,0:T(8,128)(2,1)S(1)}, bf16[1,2,512,768]{3,2,1,0:T(8,128)(2,1)}, u32[]{:S(2)}) copy-start(bf16[1,2,512,768]{3,2,1,0:T(8,128)(2,1)} %param.5) | copy-start | bytes 4718596
  8.0 61.0 %collective-permute-start.2 = (bf16[3072,768]{1,0:T(8,128)(2,1)}, bf16[3072,768]{1,0:T(8,128)(2,1)}, u32[]{:S(2)}, u32[]{:S(2)}) collective-permute-start(bf16[3072,768]{1,0:T(8,128)(2,1)} %get-tuple-element.9), channel_id=1, source_target_pairs={{0,1},{1,0},{2,3},{3,2},{4,5},{5,4},{6,7},{7,6},{8,9},{9,8},{10,11... | collective-permute-start | bytes 14155784 | tf_op jit(solution)/shard_map/ppermute | solution.py:29
  8.7 39.9 %collective-permute-start = (bf16[2,512,768]{1,2,0:T(8,128)(2,1)S(1)}, bf16[2,512,768]{1,2,0:T(8,128)(2,1)S(1)}, u32[]{:S(2)}, u32[]{:S(2)}) collective-permute-start(bf16[2,512,768]{1,2,0:T(8,128)(2,1)S(1)} %bitcast.57), channel_id=1, source_target_pairs={{0,248},{1,249},{2,250},{3,251},{4,252},{5,253},{6,254},{7,255},{8... | collective-permute-start | bytes 4718600 | tf_op jit(solution)/shard_map/ppermute | solution.py:29
  49.6 6.3 %copy-start.2 = (bf16[1,512,768]{1,2,0:T(8,128)(2,1)S(1)}, bf16[1,512,768]{1,2,0:T(8,128)(2,1)}, u32[]{:S(2)}) copy-start(bf16[1,512,768]{1,2,0:T(8,128)(2,1)} %copy.11) | copy-start | bytes 2359300
  55.9 4.1 %copy-start.3 = (bf16[1,64,6144]{2,1,0:T(8,128)(2,1)S(1)}, bf16[1,64,6144]{2,1,0:T(8,128)(2,1)}, u32[]{:S(2)}) copy-start(bf16[1,64,6144]{2,1,0:T(8,128)(2,1)} %param.9) | copy-start | bytes 2359300
  60.0 3.1 %collective-permute-start.1 = (bf16[512,768]{0,1:T(8,128)(2,1)S(1)}, bf16[512,768]{0,1:T(8,128)(2,1)S(1)}, u32[]{:S(2)}, u32[]{:S(2)}) collective-permute-start(bf16[512,768]{0,1:T(8,128)(2,1)S(1)} %bitcast.61), channel_id=1, source_target_pairs={{0,1},{1,0},{2,3},{3,2},{4,5},{5,4},{6,7},{7,6},{8,9},{9,8},{10,11... | collective-permute-start | bytes 2359304 | tf_op jit(solution)/shard_map/ppermute | solution.py:29
  60.1 2.8 %collective-permute-start.4 = (bf16[64,3072]{1,0:T(8,128)(2,1)S(1)}, bf16[64,3072]{1,0:T(8,128)(2,1)S(1)}, u32[]{:S(2)}, u32[]{:S(2)}) collective-permute-start(bf16[64,3072]{1,0:T(8,128)(2,1)S(1)} %get-tuple-element.14), channel_id=1, source_target_pairs={{0,1},{1,0},{2,3},{3,2},{4,5},{5,4},{6,7},{7,6},{8,9},{9,8},{10,11... | collective-permute-start | bytes 1179656 | tf_op jit(solution)/shard_map/ppermute | solution.py:29
  74.0 16.5 %collective-permute-start.6 = (bf16[128,768]{1,0:T(8,128)(2,1)S(1)}, bf16[128,768]{1,0:T(8,128)(2,1)S(1)}, u32[]{:S(2)}, u32[]{:S(2)}) collective-permute-start(bf16[128,768]{1,0:T(8,128)(2,1)S(1)} %get-tuple-element.22), channel_id=1, source_target_pairs={{0,6},{1,7},{2,0},{3,1},{4,2},{5,3},{6,4},{7,5},{8,14},{9,15},{10,... | collective-permute-start | bytes 589832 | tf_op jit(solution)/shard_map/ppermute | solution.py:29
  79.5 19.4 %collective-permute-start.3 = (bf16[128,768]{1,0:T(8,128)(2,1)S(1)}, bf16[128,768]{1,0:T(8,128)(2,1)S(1)}, u32[]{:S(2)}, u32[]{:S(2)}) collective-permute-start(bf16[128,768]{1,0:T(8,128)(2,1)S(1)} %get-tuple-element.21), channel_id=1, source_target_pairs={{0,2},{1,3},{2,4},{3,5},{4,6},{5,7},{6,0},{7,1},{8,10},{9,11},{10,... | collective-permute-start | bytes 589832 | tf_op jit(solution)/shard_map/ppermute | solution.py:29
  80.4 12.8 %collective-permute-start.11 = (bf16[128,768]{1,0:T(8,128)(2,1)S(1)}, bf16[128,768]{1,0:T(8,128)(2,1)S(1)}, u32[]{:S(2)}, u32[]{:S(2)}) collective-permute-start(bf16[128,768]{1,0:T(8,128)(2,1)S(1)} %get-tuple-element.20), channel_id=1, source_target_pairs={{0,6},{1,7},{2,0},{3,1},{4,2},{5,3},{6,4},{7,5},{8,14},{9,15},{10,... | collective-permute-start | bytes 589832 | tf_op jit(solution)/shard_map/ppermute | solution.py:29
  84.6 17.6 %collective-permute-start.9 = (bf16[128,768]{1,0:T(8,128)(2,1)S(1)}, bf16[128,768]{1,0:T(8,128)(2,1)S(1)}, u32[]{:S(2)}, u32[]{:S(2)}) collective-permute-start(bf16[128,768]{1,0:T(8,128)(2,1)S(1)} %get-tuple-element.19), channel_id=1, source_target_pairs={{0,2},{1,3},{2,4},{3,5},{4,6},{5,7},{6,0},{7,1},{8,10},{9,11},{10,... | collective-permute-start | bytes 589832 | tf_op jit(solution)/shard_map/ppermute | solution.py:29
  85.5 26.4 %collective-permute-start.16 = (bf16[128,768]{1,0:T(8,128)(2,1)S(1)}, bf16[128,768]{1,0:T(8,128)(2,1)S(1)}, u32[]{:S(2)}, u32[]{:S(2)}) collective-permute-start(bf16[128,768]{1,0:T(8,128)(2,1)S(1)} %get-tuple-element.18), channel_id=1, source_target_pairs={{0,6},{1,7},{2,0},{3,1},{4,2},{5,3},{6,4},{7,5},{8,14},{9,15},{10,... | collective-permute-start | bytes 589832 | tf_op jit(solution)/shard_map/ppermute | solution.py:29
  90.5 23.5 %collective-permute-start.14 = (bf16[128,768]{1,0:T(8,128)(2,1)S(1)}, bf16[128,768]{1,0:T(8,128)(2,1)S(1)}, u32[]{:S(2)}, u32[]{:S(2)}) collective-permute-start(bf16[128,768]{1,0:T(8,128)(2,1)S(1)} %get-tuple-element.17), channel_id=1, source_target_pairs={{0,2},{1,3},{2,4},{3,5},{4,6},{5,7},{6,0},{7,1},{8,10},{9,11},{10,... | collective-permute-start | bytes 589832 | tf_op jit(solution)/shard_map/ppermute | solution.py:29
  93.2 22.7 %collective-permute-start.21 = (bf16[128,768]{1,0:T(8,128)(2,1)S(1)}, bf16[128,768]{1,0:T(8,128)(2,1)S(1)}, u32[]{:S(2)}, u32[]{:S(2)}) collective-permute-start(bf16[128,768]{1,0:T(8,128)(2,1)S(1)} %get-tuple-element.16), channel_id=1, source_target_pairs={{0,6},{1,7},{2,0},{3,1},{4,2},{5,3},{6,4},{7,5},{8,14},{9,15},{10,... | collective-permute-start | bytes 589832 | tf_op jit(solution)/shard_map/ppermute | solution.py:29
  98.9 19.1 %collective-permute-start.19 = (bf16[128,768]{1,0:T(8,128)(2,1)S(1)}, bf16[128,768]{1,0:T(8,128)(2,1)S(1)}, u32[]{:S(2)}, u32[]{:S(2)}) collective-permute-start(bf16[128,768]{1,0:T(8,128)(2,1)S(1)} %get-tuple-element.15), channel_id=1, source_target_pairs={{0,2},{1,3},{2,4},{3,5},{4,6},{5,7},{6,0},{7,1},{8,10},{9,11},{10,... | collective-permute-start | bytes 589832 | tf_op jit(solution)/shard_map/ppermute | solution.py:29
  102.2 18.7 %collective-permute-start.7 = (bf16[128,768]{1,0:T(8,128)(2,1)S(1)}, bf16[128,768]{1,0:T(8,128)(2,1)S(1)}, u32[]{:S(2)}, u32[]{:S(2)}) collective-permute-start(bf16[128,768]{1,0:T(8,128)(2,1)S(1)} %fusion.27), channel_id=1, source_target_pairs={{0,14},{1,15},{2,8},{3,9},{4,10},{5,11},{6,12},{7,13},{8,0},{9,1},... | collective-permute-start | bytes 589832 | tf_op jit(solution)/shard_map/ppermute | solution.py:29
  111.8 10.2 %collective-permute-start.5 = (bf16[128,768]{1,0:T(8,128)(2,1)S(1)}, bf16[128,768]{1,0:T(8,128)(2,1)S(1)}, u32[]{:S(2)}, u32[]{:S(2)}) collective-permute-start(bf16[128,768]{1,0:T(8,128)(2,1)S(1)} %fusion.28), channel_id=1, source_target_pairs={{0,8},{1,9},{2,10},{3,11},{4,12},{5,13},{6,14},{7,15},{8,2},{9,3},... | collective-permute-start | bytes 589832 | tf_op jit(solution)/shard_map/ppermute | solution.py:29
  114.0 10.3 %collective-permute-start.12 = (bf16[128,768]{1,0:T(8,128)(2,1)S(1)}, bf16[128,768]{1,0:T(8,128)(2,1)S(1)}, u32[]{:S(2)}, u32[]{:S(2)}) collective-permute-start(bf16[128,768]{1,0:T(8,128)(2,1)S(1)} %fusion.25), channel_id=1, source_target_pairs={{0,14},{1,15},{2,8},{3,9},{4,10},{5,11},{6,12},{7,13},{8,0},{9,1},... | collective-permute-start | bytes 589832 | tf_op jit(solution)/shard_map/ppermute | solution.py:29
  115.9 10.3 %collective-permute-start.10 = (bf16[128,768]{1,0:T(8,128)(2,1)S(1)}, bf16[128,768]{1,0:T(8,128)(2,1)S(1)}, u32[]{:S(2)}, u32[]{:S(2)}) collective-permute-start(bf16[128,768]{1,0:T(8,128)(2,1)S(1)} %fusion.26), channel_id=1, source_target_pairs={{0,8},{1,9},{2,10},{3,11},{4,12},{5,13},{6,14},{7,15},{8,2},{9,3},... | collective-permute-start | bytes 589832 | tf_op jit(solution)/shard_map/ppermute | solution.py:29
  118.0 10.2 %collective-permute-start.17 = (bf16[128,768]{1,0:T(8,128)(2,1)S(1)}, bf16[128,768]{1,0:T(8,128)(2,1)S(1)}, u32[]{:S(2)}, u32[]{:S(2)}) collective-permute-start(bf16[128,768]{1,0:T(8,128)(2,1)S(1)} %fusion.23), channel_id=1, source_target_pairs={{0,14},{1,15},{2,8},{3,9},{4,10},{5,11},{6,12},{7,13},{8,0},{9,1},... | collective-permute-start | bytes 589832 | tf_op jit(solution)/shard_map/ppermute | solution.py:29
  120.8 9.6 %collective-permute-start.15 = (bf16[128,768]{1,0:T(8,128)(2,1)S(1)}, bf16[128,768]{1,0:T(8,128)(2,1)S(1)}, u32[]{:S(2)}, u32[]{:S(2)}) collective-permute-start(bf16[128,768]{1,0:T(8,128)(2,1)S(1)} %fusion.24), channel_id=1, source_target_pairs={{0,8},{1,9},{2,10},{3,11},{4,12},{5,13},{6,14},{7,15},{8,2},{9,3},... | collective-permute-start | bytes 589832 | tf_op jit(solution)/shard_map/ppermute | solution.py:29
  122.0 10.4 %collective-permute-start.22 = (bf16[128,768]{1,0:T(8,128)(2,1)S(1)}, bf16[128,768]{1,0:T(8,128)(2,1)S(1)}, u32[]{:S(2)}, u32[]{:S(2)}) collective-permute-start(bf16[128,768]{1,0:T(8,128)(2,1)S(1)} %fusion.21), channel_id=1, source_target_pairs={{0,14},{1,15},{2,8},{3,9},{4,10},{5,11},{6,12},{7,13},{8,0},{9,1},... | collective-permute-start | bytes 589832 | tf_op jit(solution)/shard_map/ppermute | solution.py:29
  124.3 9.2 %collective-permute-start.20 = (bf16[128,768]{1,0:T(8,128)(2,1)S(1)}, bf16[128,768]{1,0:T(8,128)(2,1)S(1)}, u32[]{:S(2)}, u32[]{:S(2)}) collective-permute-start(bf16[128,768]{1,0:T(8,128)(2,1)S(1)} %fusion.22), channel_id=1, source_target_pairs={{0,8},{1,9},{2,10},{3,11},{4,12},{5,13},{6,14},{7,15},{8,2},{9,3},... | collective-permute-start | bytes 589832 | tf_op jit(solution)/shard_map/ppermute | solution.py:29
  126.2 15.1 %collective-permute-start.24 = (bf16[64,768]{1,0:T(8,128)(2,1)S(1)}, bf16[64,768]{1,0:T(8,128)(2,1)S(1)}, u32[]{:S(2)}, u32[]{:S(2)}) collective-permute-start(bf16[64,768]{1,0:T(8,128)(2,1)S(1)} %get-tuple-element.37), channel_id=1, source_target_pairs={{0,1},{1,0},{2,3},{3,2},{4,5},{5,4},{6,7},{7,6},{16,17},{17,16},{1... | collective-permute-start | bytes 294920 | tf_op jit(solution)/shard_map/ppermute | solution.py:29
  128.2 15.6 %collective-permute-start.25 = (bf16[64,768]{1,0:T(8,128)(2,1)S(1)}, bf16[64,768]{1,0:T(8,128)(2,1)S(1)}, u32[]{:S(2)}, u32[]{:S(2)}) collective-permute-start(bf16[64,768]{1,0:T(8,128)(2,1)S(1)} %get-tuple-element.35), channel_id=1, source_target_pairs={{0,1},{1,0},{2,3},{3,2},{4,5},{5,4},{6,7},{7,6},{16,17},{17,16},{1... | collective-permute-start | bytes 294920 | tf_op jit(solution)/shard_map/ppermute | solution.py:29
  130.5 16.3 %collective-permute-start.26 = (bf16[64,768]{1,0:T(8,128)(2,1)S(1)}, bf16[64,768]{1,0:T(8,128)(2,1)S(1)}, u32[]{:S(2)}, u32[]{:S(2)}) collective-permute-start(bf16[64,768]{1,0:T(8,128)(2,1)S(1)} %get-tuple-element.33), channel_id=1, source_target_pairs={{0,1},{1,0},{2,3},{3,2},{4,5},{5,4},{6,7},{7,6},{16,17},{17,16},{1... | collective-permute-start | bytes 294920 | tf_op jit(solution)/shard_map/ppermute | solution.py:29
  133.6 15.4 %collective-permute-start.27 = (bf16[64,768]{1,0:T(8,128)(2,1)S(1)}, bf16[64,768]{1,0:T(8,128)(2,1)S(1)}, u32[]{:S(2)}, u32[]{:S(2)}) collective-permute-start(bf16[64,768]{1,0:T(8,128)(2,1)S(1)} %get-tuple-element.31), channel_id=1, source_target_pairs={{0,1},{1,0},{2,3},{3,2},{4,5},{5,4},{6,7},{7,6},{16,17},{17,16},{1... | collective-permute-start | bytes 294920 | tf_op jit(solution)/shard_map/ppermute | solution.py:29
  139.4 9.7 %collective-permute-start.8 = (bf16[64,768]{1,0:T(8,128)(2,1)S(1)}, bf16[64,768]{1,0:T(8,128)(2,1)S(1)}, u32[]{:S(2)}, u32[]{:S(2)}) collective-permute-start(bf16[64,768]{1,0:T(8,128)(2,1)S(1)} %get-tuple-element.38), channel_id=1, source_target_pairs={{24,8},{25,9},{26,10},{27,11},{28,12},{29,13},{30,14},{31,15},{40,... | collective-permute-start | bytes 294920 | tf_op jit(solution)/shard_map/ppermute | solution.py:29
  141.3 9.0 %collective-permute-start.13 = (bf16[64,768]{1,0:T(8,128)(2,1)S(1)}, bf16[64,768]{1,0:T(8,128)(2,1)S(1)}, u32[]{:S(2)}, u32[]{:S(2)}) collective-permute-start(bf16[64,768]{1,0:T(8,128)(2,1)S(1)} %get-tuple-element.36), channel_id=1, source_target_pairs={{24,8},{25,9},{26,10},{27,11},{28,12},{29,13},{30,14},{31,15},{40,... | collective-permute-start | bytes 294920 | tf_op jit(solution)/shard_map/ppermute | solution.py:29
  143.8 8.6 %collective-permute-start.18 = (bf16[64,768]{1,0:T(8,128)(2,1)S(1)}, bf16[64,768]{1,0:T(8,128)(2,1)S(1)}, u32[]{:S(2)}, u32[]{:S(2)}) collective-permute-start(bf16[64,768]{1,0:T(8,128)(2,1)S(1)} %get-tuple-element.34), channel_id=1, source_target_pairs={{24,8},{25,9},{26,10},{27,11},{28,12},{29,13},{30,14},{31,15},{40,... | collective-permute-start | bytes 294920 | tf_op jit(solution)/shard_map/ppermute | solution.py:29
  146.8 8.6 %collective-permute-start.23 = (bf16[64,768]{1,0:T(8,128)(2,1)S(1)}, bf16[64,768]{1,0:T(8,128)(2,1)S(1)}, u32[]{:S(2)}, u32[]{:S(2)}) collective-permute-start(bf16[64,768]{1,0:T(8,128)(2,1)S(1)} %get-tuple-element.32), channel_id=1, source_target_pairs={{24,8},{25,9},{26,10},{27,11},{28,12},{29,13},{30,14},{31,15},{40,... | collective-permute-start | bytes 294920 | tf_op jit(solution)/shard_map/ppermute | solution.py:29

commit v2 on v0

v2 whole, which is shorter than its diff:
```python
import functools

import jax
import jax.numpy as jnp
from jax import lax
from jax.experimental import pallas as pl
from jax.experimental.pallas import tpu as pltpu
from jax.sharding import PartitionSpec as P

HD = 128
TOK = 512
FEAT = 6144
AXES = ("section", "tensor")
GROUPS = ((0, 3), (3, 3))
PIECES = 4
TILE = 768
BLOCK = 128
BLOCKS = TOK // BLOCK
NT = (((1,), (1,)), ((), ()))
NN = (((1,), (0,)), ((), ()))
VMEM = 48 * 1024 * 1024


def place_of(device):
    section, tensor = divmod(device, 8)
    return section // 8, section // 2 % 4, tensor // 2 * 2 + section % 2, tensor % 2


def device_at(y, x, z, core):
    section = (y % 4) * 8 + (x % 4) * 2 + z % 2
    return section * 8 + z % 8 // 2 * 2 + core


def sent(value, target):
    pairs = []
    for device in range(256):
        place = target(*place_of(device))
        if place is not None:
            pairs.append((device, device_at(*place)))
    return lax.ppermute(value, AXES, pairs)


def mirror(y, x, z, core):
    return 3 - y, 3 - x, z ^ 1, core


def other_core(y, x, z, core):
    return y, x, z, 1 - core


def along_z(by):
    return lambda y, x, z, core: (y, x, z + by, core)


def to_previous(by):
    def target(y, x, z, core):
        if z % 2 == 1:
            return y, x, z + by, core
        if x > 0:
            return y, x - 1, z + by, core
        return (y - 1, 3, z + by, core) if y > 0 else None

    return target


def iota(shape, dim, start=0):
    return lax.broadcasted_iota(jnp.int32, shape, dim) + start


def boundaries(row):
    return [
        jnp.sum(jnp.where(row < n, 1.0, 0.0), axis=1, keepdims=True).astype(jnp.int32)
        for n in (1, 2, 3)
    ]


def starts(bounds, positions):
    found = jnp.zeros_like(positions)
    for bound in bounds:
        found = jnp.where(positions >= bound, bound, found)
    return found


def dot(left, right, dims=NN):
    return lax.dot_general(left, right, dims, preferred_element_type=jnp.float32)


def one_hot(condition):
    return jnp.where(condition, 1.0, 0.0).astype(jnp.bfloat16)


def window(n):
    low = max(n - 2, 0)
    return low, n - low + 1


def seen(bounds, n):
    low, count = window(n)
    keys = iota((count * BLOCK, BLOCK), 0, low * BLOCK)
    rows = iota((1, BLOCK), 1, n * BLOCK)
    return (keys >= starts(bounds, rows)) & (keys <= rows)


def pack_kernel(heads, place_ref, stash_ref, segment_ref, out_ref, over_ref, diagonal_ref):
    bounds = boundaries(segment_ref[pl.ds(place_ref[0], 1), :])
    below = iota((BLOCK, BLOCK), 0) < iota((BLOCK, BLOCK), 1)
    level = iota((BLOCK, BLOCK), 0) == iota((BLOCK, BLOCK), 1)
    above = iota((BLOCK, BLOCK), 0) > iota((BLOCK, BLOCK), 1)
    diagonal_ref[...] = jnp.zeros_like(diagonal_ref)
    factor = HD ** (-0.5) * 1.4426950408889634
    for n in range(BLOCKS):
        low, count = window(n)
        here = slice(n * BLOCK, (n + 1) * BLOCK)
        bias = jnp.where(seen(bounds, n), 0.0, -1e30)
        if n:
            columns = iota((1, n * BLOCK - low * BLOCK), 1, low * BLOCK)
            shifted = iota((BLOCK, 1), 0) + columns - 2 * starts(bounds, columns) - 127
            folding = one_hot((shifted & 127) == 0)
        for h in range(heads):
            features = slice(h * HD, (h + 1) * HD)
            keys = stash_ref[0, 1, low * BLOCK : (n + 1) * BLOCK, features]
            scores = dot(keys, stash_ref[0, 0, here, features], NT) + bias
            largest = jnp.max(scores, axis=0, keepdims=True)
            raised = jnp.exp2((scores - largest) * factor)
            probs = raised * (1.0 / jnp.sum(raised, axis=0, keepdims=True))
            last = probs[(count - 1) * BLOCK :]
            second = probs[(count - 2) * BLOCK : (count - 1) * BLOCK] if n else None
            first = probs[:BLOCK] if n > 1 else None
            diagonal_ref[h : h + 1, here] = jnp.sum(
                jnp.where(level, last, 0.0), axis=0, keepdims=True
            )
            kept = jnp.where(below, last, second if n else 0.0)
            out_ref[features, here] = kept.astype(jnp.bfloat16)
            if n:
                over = jnp.where(below, second, 0.0).astype(jnp.bfloat16)
                if n > 1:
                    over = jnp.concatenate(
                        [jnp.where(above, first, 0.0).astype(jnp.bfloat16), over], 0
                    )
                over_ref[features, (n - 1) * BLOCK : n * BLOCK] = dot(folding, over).astype(
                    jnp.bfloat16
                )
    wide = TOK - BLOCK
    rows = iota((wide, 1), 0, BLOCK)
    swap = one_hot(iota((wide, TOK), 1) == 2 * starts(bounds, rows) + 256 - rows)
    moved = dot(over_ref[...], swap)
    out_ref[: heads * HD, :] = (out_ref[: heads * HD, :].astype(jnp.float32) + moved).astype(
        jnp.bfloat16
    )
    out_ref[heads * HD :, :] = diagonal_ref[...].astype(jnp.bfloat16)


def unpack_kernel(heads, place_ref, packed_ref, grad_ref, segment_ref, own_ref, given_ref):
    bounds = boundaries(segment_ref[pl.ds(place_ref[1], 1), :])
    core = place_ref[2]
    base = place_ref[3]
    below = iota((BLOCK, BLOCK), 0) < iota((BLOCK, BLOCK), 1)
    level = iota((BLOCK, BLOCK), 0) == iota((BLOCK, BLOCK), 1)
    above = iota((BLOCK, BLOCK), 0) > iota((BLOCK, BLOCK), 1)
    wide = TOK - BLOCK
    queries = iota((1, wide), 1, BLOCK)
    swap = one_hot(iota((TOK, wide), 0) == 2 * starts(bounds, queries) + 256 - queries)
    over = dot(packed_ref[: heads * HD, :], swap).astype(jnp.bfloat16)
    probs = {}
    for n in range(BLOCKS):
        low, count = window(n)
        here = slice(n * BLOCK, (n + 1) * BLOCK)
        visible = seen(bounds, n)
        if n:
            rows = iota(((n - low) * BLOCK, 1), 0, low * BLOCK)
            shifted = iota((1, BLOCK), 1) + rows - 2 * starts(bounds, rows) - 127
            unfolding = one_hot((shifted & 127) == 0)
        for h in range(heads):
            features = slice(h * HD, (h + 1) * HD)
            kept = packed_ref[features, here].astype(jnp.float32)
            level_row = packed_ref[heads * HD : heads * HD + 16, here].astype(jnp.float32)[h : h + 1]
            parts = [jnp.where(below, kept, jnp.where(level, level_row, 0.0))]
            if n:
                found = dot(unfolding, over[features, (n - 1) * BLOCK : n * BLOCK])
                parts = [jnp.where(below, found[-BLOCK:], kept)] + parts
            if n > 1:
                parts = [jnp.where(above, found[:BLOCK], 0.0)] + parts
            for m, part in enumerate(parts):
                shown = jnp.where(visible[m * BLOCK : (m + 1) * BLOCK], part, 0.0)
                probs[h, low + m, n] = shown.astype(jnp.bfloat16)
    half = BLOCK // 2
    for m in range(BLOCKS):
        place = pl.multiple_of(lax.rem(m - base + BLOCKS, BLOCKS) * half, half)
        last = min(m + 3, BLOCKS)
        for h in range(heads):
            features = slice(h * HD, (h + 1) * HD)
            left = jnp.concatenate([probs[h, m, n] for n in range(m, last)], 1)
            grad = dot(left, grad_ref[0, m * BLOCK : last * BLOCK, features])
            own_ref[pl.ds(place, half), features] = jnp.where(
                core == 0, grad[:half], grad[half:]
            ).astype(jnp.bfloat16)
            given_ref[pl.ds(place, half), features] = jnp.where(
                core == 0, grad[half:], grad[:half]
            ).astype(jnp.bfloat16)


def packed_probs(place, stashed, segment_ids, first, heads):
    width = heads * HD
    return pl.pallas_call(
        functools.partial(pack_kernel, heads),
        out_shape=jax.ShapeDtypeStruct((width + 16, TOK), jnp.bfloat16),
        grid_spec=pltpu.PrefetchScalarGridSpec(
            num_scalar_prefetch=1,
            grid=(1,),
            in_specs=[
                pl.BlockSpec((1, 2, TOK, width), lambda i, p: (0, 0, 0, first // heads)),
                pl.BlockSpec((32, TOK), lambda i, p: (0, 0)),
            ],
            out_specs=pl.BlockSpec((width + 16, TOK), lambda i, p: (0, 0)),
            scratch_shapes=[
                pltpu.VMEM((width, TOK - BLOCK), jnp.bfloat16),
                pltpu.VMEM((16, TOK), jnp.float32),
            ],
        ),
        compiler_params=pltpu.CompilerParams(vmem_limit_bytes=VMEM),
    )(place, stashed, segment_ids)


def value_gradient(place, packed, grad_heads, segment_ids, first, heads):
    width = heads * HD
    out = jax.ShapeDtypeStruct((TOK // 2, width), jnp.bfloat16)
    return pl.pallas_call(
        functools.partial(unpack_kernel, heads),
        out_shape=(out, out),
        grid_spec=pltpu.PrefetchScalarGridSpec(
            num_scalar_prefetch=1,
            grid=(1,),
            in_specs=[
                pl.BlockSpec((width + 16, TOK), lambda i, p: (0, 0)),
                pl.BlockSpec((1, TOK, width), lambda i, p: (0, 0, first // heads)),
                pl.BlockSpec((32, TOK), lambda i, p: (0, 0)),
            ],
            out_specs=(
                pl.BlockSpec((TOK // 2, width), lambda i, p: (0, 0)),
                pl.BlockSpec((TOK // 2, width), lambda i, p: (0, 0)),
            ),
        ),
        compiler_params=pltpu.CompilerParams(vmem_limit_bytes=VMEM),
    )(place, packed, grad_heads, segment_ids)


def product_kernel(own_ref, taken_ref, weight_ref, other_ref, up_ref, down_ref, near_ref):
    sums = dot(own_ref[...], weight_ref[0], NT) + dot(taken_ref[...], other_ref[...], NT)
    up_ref[...] = sums[64:128].astype(jnp.bfloat16)
    down_ref[...] = sums[128:192].astype(jnp.bfloat16)
    near_ref[:64] = sums[:64]
    near_ref[64:] = sums[192:]


def products(own, taken, weight, other_weight, start, width):
    sent_shape = jax.ShapeDtypeStruct((64, width), jnp.bfloat16)
    first = start // TILE
    rows, heads = own.shape
    return pl.pallas_call(
        product_kernel,
        out_shape=(sent_shape, sent_shape, jax.ShapeDtypeStruct((128, width), jnp.float32)),
        grid=(width // TILE,),
        in_specs=[
            pl.BlockSpec((rows, heads), lambda i: (0, 0)),
            pl.BlockSpec((rows, heads), lambda i: (0, 0)),
            pl.BlockSpec((1, TILE, heads), lambda i: (0, first + i, 0)),
            pl.BlockSpec((TILE, heads), lambda i: (first + i, 0)),
        ],
        out_specs=(
            pl.BlockSpec((64, TILE), lambda i: (0, i)),
            pl.BlockSpec((64, TILE), lambda i: (0, i)),
            pl.BlockSpec((128, TILE), lambda i: (0, i)),
        ),
        compiler_params=pltpu.CompilerParams(vmem_limit_bytes=VMEM),
    )(own, taken, weight, other_weight)


def body(stashed_qk, grad_heads, segment_ids, w_value, grad_in):
    section = lax.axis_index("section")
    tensor = lax.axis_index("tensor")
    z_low, z_high, core = section % 2, tensor // 2, tensor % 2
    piece = FEAT // PIECES
    base = (z_high + z_low) % BLOCKS
    place = jnp.stack([31 - section, section, core, base]).astype(jnp.int32)

    weight = w_value[0]
    other_weight = sent(weight, other_core)
    packed = [
        sent(packed_probs(place, stashed_qk, segment_ids, *group), mirror) for group in GROUPS
    ]
    own, taken = [], []
    for group, probs in zip(GROUPS, packed):
        kept, given = value_gradient(place, probs, grad_heads, segment_ids, *group)
        own.append(kept)
        taken.append(sent(given, other_core))
    own = jnp.concatenate(own, 1)
    taken = jnp.concatenate(taken, 1)

    far, near = [], []
    for n in range(PIECES):
        up, down, rest = products(own, taken, w_value, other_weight, n * piece, piece)
        far.append((sent(up, along_z(2)), sent(down, along_z(-2))))
        near.append(rest)
    pieces = []
    for n in range(PIECES):
        added = grad_in[0][:, n * piece : (n + 1) * piece].astype(jnp.float32)
        up = near[n][:64] + far[n][0].astype(jnp.float32) + jnp.where(z_low == 0, added, 0.0)
        down = near[n][64:] + far[n][1].astype(jnp.float32) + jnp.where(z_low == 1, added, 0.0)
        risen = sent(up.astype(jnp.bfloat16), to_previous(1))
        fallen = sent(down.astype(jnp.bfloat16), to_previous(-1))
        pieces.append((risen.astype(jnp.float32) + fallen.astype(jnp.float32)).astype(jnp.bfloat16))
    return jnp.concatenate(pieces, 1)[None]


def solution(mesh):
    in_specs = (
        P("section", None, None, "tensor"),
        P("section", None, "tensor"),
        P(),
        P("section", None, "tensor"),
        P("section", "tensor", None),
    )
    out_specs = P("section", "tensor", None)
    return jax.shard_map(body, mesh=mesh, in_specs=in_specs, out_specs=out_specs, check_vma=False)
```

time: 317 us -> 112 us (0.35)
  waiting for transfers between devices: 262 us -> 35.9 us
  starting transfers between devices: 12.7 us -> 46.9 us
  Pallas kernels: 0 us -> 22.7 us
  matrix products: 20.9 us -> 0 us
  between operations: 13.4 us -> 0.28 us
    ppermute x6 -> x21, waiting for transfers between devices: 183 us -> 35.9 us  [sent(): return lax.ppermute(value, AXES, pairs)]
    reduce_scatter x1 -> x0, waiting for transfers between devices: 79.3 us -> none  [body(): lax.psum_scatter(lax.dot_general(value_grad, weight, (((1,), (1,)), ((),...]
    ppermute x6 -> x21, starting transfers between devices: 12.7 us -> 46.9 us  [sent(): return lax.ppermute(value, AXES, pairs)]
    pallas_call x0 -> x8, Pallas kernels: none -> 22.7 us  [the longest x4 13.4 us: products(): pl.pallas_call(product_kernel, out_shape=(sent_shape, sent_shape, jax.Sha...]
    dot_general x2 -> x0, matrix products: 14.7 us -> none  [the longest x1 10.7 us: body(): lax.dot_general(value_grad, weight, (((1,), (1,)), ((), ())), preferred_e...]
    sub x1 -> x0, matrix products: 6.22 us -> none  [value_gradient(): raised = jnp.exp(scores - largest)]
  transfers between devices with their start and end apart: 7 -> 21, of which waited for: 7 -> 9; matrix products, arithmetic and copies ran while one was open for 1% -> 2% of each run, Pallas kernels for 0% -> 17%
where the time goes in v2:
time: 112 us; the launch traced here: 111 us
  starting transfers between devices  46.9 us (42%)
  waiting for transfers between devices  35.9 us (32%)
  Pallas kernels  22.7 us (20%)
  other arithmetic  2.77 us (2%)
  local copies, waits for them, and re-layouts  2.37 us (2%)
    ppermute x21, starting transfers between devices, sent(): return lax.ppermute(value, AXES, pairs)  46.9 us
    ppermute x21, waiting for transfers between devices, sent(): return lax.ppermute(value, AXES, pairs)  35.9 us
    pallas_call x4, Pallas kernels, products(): pl.pallas_call(product_kernel, out_shape=(sent_shape, sent_shape, jax.Sha...  13.4 us
    pallas_call x2, Pallas kernels, packed_probs(): pl.pallas_call(functools.partial(pack_kernel, heads), out_shape=jax.Shape...  6.04 us
    pallas_call x2, Pallas kernels, value_gradient(): pl.pallas_call(functools.partial(unpack_kernel, heads), out_shape=(out, o...  3.24 us
    unnamed x12, local copies, waits for them, and re-layouts  2.31 us
  transfers between devices with their start and end apart: 21, of which 9 were waited for; matrix products, arithmetic and copies ran while one was open for 2% of the time, Pallas kernels for 17%

profile of v2, /device:TPU:46, one launch (start us, length us, event | category | flops | bytes accessed | tf_op | source)
XLA Modules:
  0.0 111.0 jit_solution(13577906928626350934)
XLA Ops:
  0.1 1.4 %copy-done = bf16[1,2,512,768]{3,2,1,0:T(8,128)(2,1)S(1)} copy-done((bf16[1,2,512,768]{3,2,1,0:T(8,128)(2,1)S(1)}, bf16[1,2,512,768]{3,2,1,0:T(8,128)(2,1)}, u32[]{:S(2)}) %copy-start) | copy-done | bytes 1572888
  2.3 3.0 %shard_map.55 = bf16[400,512]{1,0:T(8,128)(2,1)S(1)} custom-call(s32[4]{0:T(128)S(1)} %pad_add_fusion.place_ref, bf16[1,2,512,768]{3,2,1,0:T(8,128)(2,1)S(1)} %copy-done, s32[32,512]{1,0:T(8,128)S(1)} %copy-done.2), custom_call_target="tpu_custom_call" | custom-call | tf_op jit(solution)/shard_map/pallas_call | solution.py:204
  6.5 3.0 %shard_map.57 = bf16[400,512]{1,0:T(8,128)(2,1)S(1)} custom-call(s32[4]{0:T(128)S(1)} %pad_add_fusion.place_ref, bf16[1,2,512,768]{3,2,1,0:T(8,128)(2,1)S(1)} %copy-done, s32[32,512]{1,0:T(8,128)S(1)} %copy-done.2), custom_call_target="tpu_custom_call" | custom-call | tf_op jit(solution)/shard_map/pallas_call | solution.py:204
  9.5 4.1 %collective-permute-start.1 = (bf16[400,512]{1,0:T(8,128)(2,1)S(1)}, bf16[400,512]{1,0:T(8,128)(2,1)S(1)}, u32[]{:S(2)}, u32[]{:S(2)}) collective-permute-start(bf16[400,512]{1,0:T(8,128)(2,1)S(1)} %shard_map.57), channel_id=1, source_target_pairs={{0,248},{1,249},{2,250},{3,251},{4,252},{5,253},{6,254},{7,255},{8... | collective-permute-start | bytes 1228808 | tf_op jit(solution)/shard_map/ppermute | solution.py:40
  13.6 7.1 %collective-permute-done.packed_ref = bf16[400,512]{1,0:T(8,128)(2,1)S(1)} collective-permute-done((bf16[400,512]{1,0:T(8,128)(2,1)S(1)}, bf16[400,512]{1,0:T(8,128)(2,1)S(1)}, u32[]{:S(2)}, u32[]{:S(2)}) %collective-permute-start) | collective-permute-done | bytes 409632 | tf_op jit(solution)/shard_map/ppermute | solution.py:40
  20.7 1.6 %shard_map.56 = (bf16[256,384]{1,0:T(8,128)(2,1)S(1)}, bf16[256,384]{1,0:T(8,128)(2,1)S(1)}) custom-call(s32[4]{0:T(128)S(1)} %pad_add_fusion.place_ref, bf16[400,512]{1,0:T(8,128)(2,1)S(1)} %collective-permute-done.packed_ref, bf16[1,512,768]{2,1,0:T(8,128)(2,1)S(1)} %copy-done.1, s32[32,512]{1,0:T(8,128)S(1)} %copy-done.3), custom_call_target="tpu_custom_call" | custom-call | tf_op jit(solution)/shard_map/pallas_call | solution.py:227
  22.5 6.7 %collective-permute-done.1.packed_ref = bf16[400,512]{1,0:T(8,128)(2,1)S(1)} collective-permute-done((bf16[400,512]{1,0:T(8,128)(2,1)S(1)}, bf16[400,512]{1,0:T(8,128)(2,1)S(1)}, u32[]{:S(2)}, u32[]{:S(2)}) %collective-permute-start.1) | collective-permute-done | bytes 409632 | tf_op jit(solution)/shard_map/ppermute | solution.py:40
  29.1 1.6 %shard_map.58 = (bf16[256,384]{1,0:T(8,128)(2,1)S(1)}, bf16[256,384]{1,0:T(8,128)(2,1)S(1)}) custom-call(s32[4]{0:T(128)S(1)} %pad_add_fusion.place_ref, bf16[400,512]{1,0:T(8,128)(2,1)S(1)} %collective-permute-done.1.packed_ref, bf16[1,512,768]{2,1,0:T(8,128)(2,1)S(1)} %copy-done.1, s32[32,512]{1,0:T(8,128)S(1)} %copy-done.3), custom_call_target="tpu_custom_call" | custom-call | tf_op jit(solution)/shard_map/pallas_call | solution.py:227
  32.3 3.4 %shard_map.62 = (bf16[64,1536]{1,0:T(8,128)(2,1)S(1)}, bf16[64,1536]{1,0:T(8,128)(2,1)S(1)}, f32[128,1536]{1,0:T(8,128)S(1)}) custom-call(bf16[256,768]{1,0:T(8,128)(2,1)S(1)} %constant_dynamic-update-slice_fusion.own_ref, bf16[256,768]{1,0:T(8,128)(2,1)S(1)} %constant_dynamic-update-slice_fusion.2.taken_ref, bf16[1,6144,768]{2,1,0:T(8,128)(2,1)} %weight_ref.7, ...), custom_call_target="tpu_custom_call" | custom-call | tf_op jit(solution)/shard_map/pallas_call | solution.py:259
  35.7 3.3 %collective-permute-start.17 = (bf16[64,1536]{1,0:T(8,128)(2,1)S(1)}, bf16[64,1536]{1,0:T(8,128)(2,1)S(1)}, u32[]{:S(2)}, u32[]{:S(2)}) collective-permute-start(bf16[64,1536]{1,0:T(8,128)(2,1)S(1)} %get-tuple-element.35), channel_id=1, source_target_pairs={{0,2},{1,3},{2,4},{3,5},{4,6},{5,7},{6,0},{7,1},{8,10},{9,11},{10,... | collective-permute-start | bytes 589832 | tf_op jit(solution)/shard_map/ppermute | solution.py:40
  39.0 2.2 %collective-permute-start.19 = (bf16[64,1536]{1,0:T(8,128)(2,1)S(1)}, bf16[64,1536]{1,0:T(8,128)(2,1)S(1)}, u32[]{:S(2)}, u32[]{:S(2)}) collective-permute-start(bf16[64,1536]{1,0:T(8,128)(2,1)S(1)} %get-tuple-element.36), channel_id=1, source_target_pairs={{0,6},{1,7},{2,0},{3,1},{4,2},{5,3},{6,4},{7,5},{8,14},{9,15},{10,... | collective-permute-start | bytes 589832 | tf_op jit(solution)/shard_map/ppermute | solution.py:40
  41.3 3.4 %shard_map.61 = (bf16[64,1536]{1,0:T(8,128)(2,1)S(1)}, bf16[64,1536]{1,0:T(8,128)(2,1)S(1)}, f32[128,1536]{1,0:T(8,128)S(1)}) custom-call(bf16[256,768]{1,0:T(8,128)(2,1)S(1)} %constant_dynamic-update-slice_fusion.own_ref, bf16[256,768]{1,0:T(8,128)(2,1)S(1)} %constant_dynamic-update-slice_fusion.2.taken_ref, bf16[1,6144,768]{2,1,0:T(8,128)(2,1)} %weight_ref.7, ...), custom_call_target="tpu_custom_call" | custom-call | tf_op jit(solution)/shard_map/pallas_call | solution.py:259
  44.6 1.6 %collective-permute-start.13 = (bf16[64,1536]{1,0:T(8,128)(2,1)S(1)}, bf16[64,1536]{1,0:T(8,128)(2,1)}, u32[]{:S(2)}, u32[]{:S(2)}) collective-permute-start(bf16[64,1536]{1,0:T(8,128)(2,1)S(1)} %get-tuple-element.32), channel_id=1, source_target_pairs={{0,2},{1,3},{2,4},{3,5},{4,6},{5,7},{6,0},{7,1},{8,10},{9,11},{10,... | collective-permute-start | bytes 589832 | tf_op jit(solution)/shard_map/ppermute | solution.py:40
  46.3 2.8 %collective-permute-start.15 = (bf16[64,1536]{1,0:T(8,128)(2,1)S(1)}, bf16[64,1536]{1,0:T(8,128)(2,1)}, u32[]{:S(2)}, u32[]{:S(2)}) collective-permute-start(bf16[64,1536]{1,0:T(8,128)(2,1)S(1)} %get-tuple-element.33), channel_id=1, source_target_pairs={{0,6},{1,7},{2,0},{3,1},{4,2},{5,3},{6,4},{7,5},{8,14},{9,15},{10,... | collective-permute-start | bytes 589832 | tf_op jit(solution)/shard_map/ppermute | solution.py:40
  49.0 3.4 %shard_map.60 = (bf16[64,1536]{1,0:T(8,128)(2,1)S(1)}, bf16[64,1536]{1,0:T(8,128)(2,1)S(1)}, f32[128,1536]{1,0:T(8,128)S(1)}) custom-call(bf16[256,768]{1,0:T(8,128)(2,1)S(1)} %constant_dynamic-update-slice_fusion.own_ref, bf16[256,768]{1,0:T(8,128)(2,1)S(1)} %constant_dynamic-update-slice_fusion.2.taken_ref, bf16[1,6144,768]{2,1,0:T(8,128)(2,1)} %weight_ref.7, ...), custom_call_target="tpu_custom_call" | custom-call | tf_op jit(solution)/shard_map/pallas_call | solution.py:259
  52.4 1.4 %collective-permute-start.9 = (bf16[64,1536]{1,0:T(8,128)(2,1)S(1)}, bf16[64,1536]{1,0:T(8,128)(2,1)S(1)}, u32[]{:S(2)}, u32[]{:S(2)}) collective-permute-start(bf16[64,1536]{1,0:T(8,128)(2,1)S(1)} %get-tuple-element.29), channel_id=1, source_target_pairs={{0,2},{1,3},{2,4},{3,5},{4,6},{5,7},{6,0},{7,1},{8,10},{9,11},{10,... | collective-permute-start | bytes 589832 | tf_op jit(solution)/shard_map/ppermute | solution.py:40
  53.9 3.3 %shard_map.59 = (bf16[64,1536]{1,0:T(8,128)(2,1)S(1)}, bf16[64,1536]{1,0:T(8,128)(2,1)S(1)}, f32[128,1536]{1,0:T(8,128)S(1)}) custom-call(bf16[256,768]{1,0:T(8,128)(2,1)S(1)} %constant_dynamic-update-slice_fusion.own_ref, bf16[256,768]{1,0:T(8,128)(2,1)S(1)} %constant_dynamic-update-slice_fusion.2.taken_ref, bf16[1,6144,768]{2,1,0:T(8,128)(2,1)} %weight_ref.7, ...), custom_call_target="tpu_custom_call" | custom-call | tf_op jit(solution)/shard_map/pallas_call | solution.py:259
  57.2 2.9 %collective-permute-start.11 = (bf16[64,1536]{1,0:T(8,128)(2,1)S(1)}, bf16[64,1536]{1,0:T(8,128)(2,1)S(1)}, u32[]{:S(2)}, u32[]{:S(2)}) collective-permute-start(bf16[64,1536]{1,0:T(8,128)(2,1)S(1)} %get-tuple-element.30), channel_id=1, source_target_pairs={{0,6},{1,7},{2,0},{3,1},{4,2},{5,3},{6,4},{7,5},{8,14},{9,15},{10,... | collective-permute-start | bytes 589832 | tf_op jit(solution)/shard_map/ppermute | solution.py:40
  60.1 1.5 %collective-permute-start.5 = (bf16[64,1536]{1,0:T(8,128)(2,1)S(1)}, bf16[64,1536]{1,0:T(8,128)(2,1)S(1)}, u32[]{:S(2)}, u32[]{:S(2)}) collective-permute-start(bf16[64,1536]{1,0:T(8,128)(2,1)S(1)} %get-tuple-element.26), channel_id=1, source_target_pairs={{0,2},{1,3},{2,4},{3,5},{4,6},{5,7},{6,0},{7,1},{8,10},{9,11},{10,... | collective-permute-start | bytes 589832 | tf_op jit(solution)/shard_map/ppermute | solution.py:40
  61.5 2.7 %collective-permute-start.7 = (bf16[64,1536]{1,0:T(8,128)(2,1)S(1)}, bf16[64,1536]{1,0:T(8,128)(2,1)S(1)}, u32[]{:S(2)}, u32[]{:S(2)}) collective-permute-start(bf16[64,1536]{1,0:T(8,128)(2,1)S(1)} %get-tuple-element.27), channel_id=1, source_target_pairs={{0,6},{1,7},{2,0},{3,1},{4,2},{5,3},{6,4},{7,5},{8,14},{9,15},{10,... | collective-permute-start | bytes 589832 | tf_op jit(solution)/shard_map/ppermute | solution.py:40
  65.5 2.8 %collective-permute-start.14 = (bf16[64,1536]{1,0:T(8,128)(2,1)S(1)}, bf16[64,1536]{1,0:T(8,128)(2,1)S(1)}, u32[]{:S(2)}, u32[]{:S(2)}) collective-permute-start(bf16[64,1536]{1,0:T(8,128)(2,1)S(1)} %get-tuple-element.41), channel_id=1, source_target_pairs={{8,2},{9,3},{10,4},{11,5},{12,6},{13,7},{14,0},{15,1},{16,8},{17,9... | collective-permute-start | bytes 589832 | tf_op jit(solution)/shard_map/ppermute | solution.py:40
  68.4 3.8 %collective-permute-done.9 = bf16[64,1536]{1,0:T(8,128)(2,1)S(1)} collective-permute-done((bf16[64,1536]{1,0:T(8,128)(2,1)S(1)}, bf16[64,1536]{1,0:T(8,128)(2,1)S(1)}, u32[]{:S(2)}, u32[]{:S(2)}) %collective-permute-start.9) | collective-permute-done | bytes 196640 | tf_op jit(solution)/shard_map/ppermute | solution.py:40
  72.2 1.9 %collective-permute-start.16 = (bf16[64,1536]{1,0:T(8,128)(2,1)S(1)}, bf16[64,1536]{1,0:T(8,128)(2,1)S(1)}, u32[]{:S(2)}, u32[]{:S(2)}) collective-permute-start(bf16[64,1536]{1,0:T(8,128)(2,1)S(1)} %get-tuple-element.42), channel_id=1, source_target_pairs={{8,0},{9,1},{10,2},{11,3},{12,4},{13,5},{14,6},{15,7},{16,14},{17,... | collective-permute-start | bytes 589832 | tf_op jit(solution)/shard_map/ppermute | solution.py:40
  74.1 3.9 %collective-permute-start.20 = (bf16[64,1536]{1,0:T(8,128)(2,1)S(1)}, bf16[64,1536]{1,0:T(8,128)(2,1)S(1)}, u32[]{:S(2)}, u32[]{:S(2)}) collective-permute-start(bf16[64,1536]{1,0:T(8,128)(2,1)S(1)} %get-tuple-element.47), channel_id=1, source_target_pairs={{8,0},{9,1},{10,2},{11,3},{12,4},{13,5},{14,6},{15,7},{16,14},{17,... | collective-permute-start | bytes 589832 | tf_op jit(solution)/shard_map/ppermute | solution.py:40
  78.0 3.2 %collective-permute-start.18 = (bf16[64,1536]{1,0:T(8,128)(2,1)S(1)}, bf16[64,1536]{1,0:T(8,128)(2,1)S(1)}, u32[]{:S(2)}, u32[]{:S(2)}) collective-permute-start(bf16[64,1536]{1,0:T(8,128)(2,1)S(1)} %get-tuple-element.48), channel_id=1, source_target_pairs={{8,2},{9,3},{10,4},{11,5},{12,6},{13,7},{14,0},{15,1},{16,8},{17,9... | collective-permute-start | bytes 589832 | tf_op jit(solution)/shard_map/ppermute | solution.py:40
  81.6 3.0 %collective-permute-start.6 = (bf16[64,1536]{1,0:T(8,128)(2,1)S(1)}, bf16[64,1536]{1,0:T(8,128)(2,1)S(1)}, u32[]{:S(2)}, u32[]{:S(2)}) collective-permute-start(bf16[64,1536]{1,0:T(8,128)(2,1)S(1)} %get-tuple-element.37), channel_id=1, source_target_pairs={{8,2},{9,3},{10,4},{11,5},{12,6},{13,7},{14,0},{15,1},{16,8},{17,9... | collective-permute-start | bytes 589832 | tf_op jit(solution)/shard_map/ppermute | solution.py:40
  84.6 1.9 %collective-permute-start.8 = (bf16[64,1536]{1,0:T(8,128)(2,1)S(1)}, bf16[64,1536]{1,0:T(8,128)(2,1)S(1)}, u32[]{:S(2)}, u32[]{:S(2)}) collective-permute-start(bf16[64,1536]{1,0:T(8,128)(2,1)S(1)} %get-tuple-element.38), channel_id=1, source_target_pairs={{8,0},{9,1},{10,2},{11,3},{12,4},{13,5},{14,6},{15,7},{16,14},{17,... | collective-permute-start | bytes 589832 | tf_op jit(solution)/shard_map/ppermute | solution.py:40
  86.5 4.4 %collective-permute-start.12 = (bf16[64,1536]{1,0:T(8,128)(2,1)S(1)}, bf16[64,1536]{1,0:T(8,128)(2,1)S(1)}, u32[]{:S(2)}, u32[]{:S(2)}) collective-permute-start(bf16[64,1536]{1,0:T(8,128)(2,1)S(1)} %get-tuple-element.45), channel_id=1, source_target_pairs={{8,0},{9,1},{10,2},{11,3},{12,4},{13,5},{14,6},{15,7},{16,14},{17,... | collective-permute-start | bytes 589832 | tf_op jit(solution)/shard_map/ppermute | solution.py:40
  91.0 2.9 %collective-permute-done.20 = bf16[64,1536]{1,0:T(8,128)(2,1)S(1)} collective-permute-done((bf16[64,1536]{1,0:T(8,128)(2,1)S(1)}, bf16[64,1536]{1,0:T(8,128)(2,1)S(1)}, u32[]{:S(2)}, u32[]{:S(2)}) %collective-permute-start.20) | collective-permute-done | bytes 196640 | tf_op jit(solution)/shard_map/ppermute | solution.py:40
  93.9 1.9 %collective-permute-start.10 = (bf16[64,1536]{1,0:T(8,128)(2,1)S(1)}, bf16[64,1536]{1,0:T(8,128)(2,1)S(1)}, u32[]{:S(2)}, u32[]{:S(2)}) collective-permute-start(bf16[64,1536]{1,0:T(8,128)(2,1)S(1)} %get-tuple-element.46), channel_id=1, source_target_pairs={{8,2},{9,3},{10,4},{11,5},{12,6},{13,7},{14,0},{15,1},{16,8},{17,9... | collective-permute-start | bytes 589832 | tf_op jit(solution)/shard_map/ppermute | solution.py:40
  96.1 8.4 %collective-permute-done.6 = bf16[64,1536]{1,0:T(8,128)(2,1)S(1)} collective-permute-done((bf16[64,1536]{1,0:T(8,128)(2,1)S(1)}, bf16[64,1536]{1,0:T(8,128)(2,1)S(1)}, u32[]{:S(2)}, u32[]{:S(2)}) %collective-permute-start.6) | collective-permute-done | bytes 196640 | tf_op jit(solution)/shard_map/ppermute | solution.py:40
  104.5 5.0 %collective-permute-done.12 = bf16[64,1536]{1,0:T(8,128)(2,1)S(1)} collective-permute-done((bf16[64,1536]{1,0:T(8,128)(2,1)S(1)}, bf16[64,1536]{1,0:T(8,128)(2,1)S(1)}, u32[]{:S(2)}, u32[]{:S(2)}) %collective-permute-start.12) | collective-permute-done | bytes 196640 | tf_op jit(solution)/shard_map/ppermute | solution.py:40
  (40 shorter events, 7.0 us)
Async XLA Ops:
  0.0 32.3 %collective-permute-start.4 = (bf16[6144,768]{1,0:T(8,128)(2,1)}, bf16[6144,768]{1,0:T(8,128)(2,1)}, u32[]{:S(2)}, u32[]{:S(2)}) collective-permute-start(bf16[6144,768]{1,0:T(8,128)(2,1)} %bitcast.8), channel_id=1, source_target_pairs={{0,1},{1,0},{2,3},{3,2},{4,5},{5,4},{6,7},{7,6},{8,9},{9,8},{10,11... | collective-permute-start | bytes 28311560 | tf_op jit(solution)/shard_map/ppermute | solution.py:40
  0.1 1.4 %copy-start = (bf16[1,2,512,768]{3,2,1,0:T(8,128)(2,1)S(1)}, bf16[1,2,512,768]{3,2,1,0:T(8,128)(2,1)}, u32[]{:S(2)}) copy-start(bf16[1,2,512,768]{3,2,1,0:T(8,128)(2,1)} %stash_ref.3) | copy-start | bytes 4718596
  1.5 0.8 copy-start.2
  2.3 18.4 %copy-start.1 = (bf16[1,512,768]{2,1,0:T(8,128)(2,1)S(1)}, bf16[1,512,768]{2,1,0:T(8,128)(2,1)}, u32[]{:S(2)}) copy-start(bf16[1,512,768]{2,1,0:T(8,128)(2,1)} %grad_ref.3) | copy-start | bytes 2359300
  2.3 18.4 %copy-start.3 = (s32[32,512]{1,0:T(8,128)S(1)}, s32[32,512]{1,0:T(8,128)}, u32[]{:S(2)}) copy-start(s32[32,512]{1,0:T(8,128)} %segment_ref.7) | copy-start | bytes 196612
  5.4 15.4 %collective-permute-start = (bf16[400,512]{1,0:T(8,128)(2,1)S(1)}, bf16[400,512]{1,0:T(8,128)(2,1)S(1)}, u32[]{:S(2)}, u32[]{:S(2)}) collective-permute-start(bf16[400,512]{1,0:T(8,128)(2,1)S(1)} %shard_map.55), channel_id=1, source_target_pairs={{0,248},{1,249},{2,250},{3,251},{4,252},{5,253},{6,254},{7,255},{8... | collective-permute-start | bytes 1228808 | tf_op jit(solution)/shard_map/ppermute | solution.py:40
  9.5 19.6 %collective-permute-start.1 = (bf16[400,512]{1,0:T(8,128)(2,1)S(1)}, bf16[400,512]{1,0:T(8,128)(2,1)S(1)}, u32[]{:S(2)}, u32[]{:S(2)}) collective-permute-start(bf16[400,512]{1,0:T(8,128)(2,1)S(1)} %shard_map.57), channel_id=1, source_target_pairs={{0,248},{1,249},{2,250},{3,251},{4,252},{5,253},{6,254},{7,255},{8... | collective-permute-start | bytes 1228808 | tf_op jit(solution)/shard_map/ppermute | solution.py:40
  22.4 8.6 %collective-permute-start.2 = (bf16[256,384]{1,0:T(8,128)(2,1)S(1)}, bf16[256,384]{1,0:T(8,128)(2,1)S(1)}, u32[]{:S(2)}, u32[]{:S(2)}) collective-permute-start(bf16[256,384]{1,0:T(8,128)(2,1)S(1)} %get-tuple-element.23), channel_id=1, source_target_pairs={{0,1},{1,0},{2,3},{3,2},{4,5},{5,4},{6,7},{7,6},{8,9},{9,8},{10,11... | collective-permute-start | bytes 589832 | tf_op jit(solution)/shard_map/ppermute | solution.py:40
  30.7 1.5 %collective-permute-start.3 = (bf16[256,384]{1,0:T(8,128)(2,1)S(1)}, bf16[256,384]{1,0:T(8,128)(2,1)S(1)}, u32[]{:S(2)}, u32[]{:S(2)}) collective-permute-start(bf16[256,384]{1,0:T(8,128)(2,1)S(1)} %get-tuple-element.24), channel_id=1, source_target_pairs={{0,1},{1,0},{2,3},{3,2},{4,5},{5,4},{6,7},{7,6},{8,9},{9,8},{10,11... | collective-permute-start | bytes 589832 | tf_op jit(solution)/shard_map/ppermute | solution.py:40
  35.7 21.5 %collective-permute-start.17 = (bf16[64,1536]{1,0:T(8,128)(2,1)S(1)}, bf16[64,1536]{1,0:T(8,128)(2,1)S(1)}, u32[]{:S(2)}, u32[]{:S(2)}) collective-permute-start(bf16[64,1536]{1,0:T(8,128)(2,1)S(1)} %get-tuple-element.35), channel_id=1, source_target_pairs={{0,2},{1,3},{2,4},{3,5},{4,6},{5,7},{6,0},{7,1},{8,10},{9,11},{10,... | collective-permute-start | bytes 589832 | tf_op jit(solution)/shard_map/ppermute | solution.py:40
  39.0 21.0 %collective-permute-start.19 = (bf16[64,1536]{1,0:T(8,128)(2,1)S(1)}, bf16[64,1536]{1,0:T(8,128)(2,1)S(1)}, u32[]{:S(2)}, u32[]{:S(2)}) collective-permute-start(bf16[64,1536]{1,0:T(8,128)(2,1)S(1)} %get-tuple-element.36), channel_id=1, source_target_pairs={{0,6},{1,7},{2,0},{3,1},{4,2},{5,3},{6,4},{7,5},{8,14},{9,15},{10,... | collective-permute-start | bytes 589832 | tf_op jit(solution)/shard_map/ppermute | solution.py:40
  44.6 16.9 %collective-permute-start.13 = (bf16[64,1536]{1,0:T(8,128)(2,1)S(1)}, bf16[64,1536]{1,0:T(8,128)(2,1)}, u32[]{:S(2)}, u32[]{:S(2)}) collective-permute-start(bf16[64,1536]{1,0:T(8,128)(2,1)S(1)} %get-tuple-element.32), channel_id=1, source_target_pairs={{0,2},{1,3},{2,4},{3,5},{4,6},{5,7},{6,0},{7,1},{8,10},{9,11},{10,... | collective-permute-start | bytes 589832 | tf_op jit(solution)/shard_map/ppermute | solution.py:40
  46.3 18.0 %collective-permute-start.15 = (bf16[64,1536]{1,0:T(8,128)(2,1)S(1)}, bf16[64,1536]{1,0:T(8,128)(2,1)}, u32[]{:S(2)}, u32[]{:S(2)}) collective-permute-start(bf16[64,1536]{1,0:T(8,128)(2,1)S(1)} %get-tuple-element.33), channel_id=1, source_target_pairs={{0,6},{1,7},{2,0},{3,1},{4,2},{5,3},{6,4},{7,5},{8,14},{9,15},{10,... | collective-permute-start | bytes 589832 | tf_op jit(solution)/shard_map/ppermute | solution.py:40
  52.4 11.8 %copy-start.4 = (bf16[1,64,6144]{2,1,0:T(8,128)(2,1)S(1)}, bf16[1,64,6144]{2,1,0:T(8,128)(2,1)}, u32[]{:S(2)}) copy-start(bf16[1,64,6144]{2,1,0:T(8,128)(2,1)} %param.9) | copy-start | bytes 2359300
  52.4 19.8 %collective-permute-start.9 = (bf16[64,1536]{1,0:T(8,128)(2,1)S(1)}, bf16[64,1536]{1,0:T(8,128)(2,1)S(1)}, u32[]{:S(2)}, u32[]{:S(2)}) collective-permute-start(bf16[64,1536]{1,0:T(8,128)(2,1)S(1)} %get-tuple-element.29), channel_id=1, source_target_pairs={{0,2},{1,3},{2,4},{3,5},{4,6},{5,7},{6,0},{7,1},{8,10},{9,11},{10,... | collective-permute-start | bytes 589832 | tf_op jit(solution)/shard_map/ppermute | solution.py:40
  57.2 16.9 %collective-permute-start.11 = (bf16[64,1536]{1,0:T(8,128)(2,1)S(1)}, bf16[64,1536]{1,0:T(8,128)(2,1)S(1)}, u32[]{:S(2)}, u32[]{:S(2)}) collective-permute-start(bf16[64,1536]{1,0:T(8,128)(2,1)S(1)} %get-tuple-element.30), channel_id=1, source_target_pairs={{0,6},{1,7},{2,0},{3,1},{4,2},{5,3},{6,4},{7,5},{8,14},{9,15},{10,... | collective-permute-start | bytes 589832 | tf_op jit(solution)/shard_map/ppermute | solution.py:40
  60.1 17.9 %collective-permute-start.5 = (bf16[64,1536]{1,0:T(8,128)(2,1)S(1)}, bf16[64,1536]{1,0:T(8,128)(2,1)S(1)}, u32[]{:S(2)}, u32[]{:S(2)}) collective-permute-start(bf16[64,1536]{1,0:T(8,128)(2,1)S(1)} %get-tuple-element.26), channel_id=1, source_target_pairs={{0,2},{1,3},{2,4},{3,5},{4,6},{5,7},{6,0},{7,1},{8,10},{9,11},{10,... | collective-permute-start | bytes 589832 | tf_op jit(solution)/shard_map/ppermute | solution.py:40
  61.5 19.7 %collective-permute-start.7 = (bf16[64,1536]{1,0:T(8,128)(2,1)S(1)}, bf16[64,1536]{1,0:T(8,128)(2,1)S(1)}, u32[]{:S(2)}, u32[]{:S(2)}) collective-permute-start(bf16[64,1536]{1,0:T(8,128)(2,1)S(1)} %get-tuple-element.27), channel_id=1, source_target_pairs={{0,6},{1,7},{2,0},{3,1},{4,2},{5,3},{6,4},{7,5},{8,14},{9,15},{10,... | collective-permute-start | bytes 589832 | tf_op jit(solution)/shard_map/ppermute | solution.py:40
  65.5 19.1 %collective-permute-start.14 = (bf16[64,1536]{1,0:T(8,128)(2,1)S(1)}, bf16[64,1536]{1,0:T(8,128)(2,1)S(1)}, u32[]{:S(2)}, u32[]{:S(2)}) collective-permute-start(bf16[64,1536]{1,0:T(8,128)(2,1)S(1)} %get-tuple-element.41), channel_id=1, source_target_pairs={{8,2},{9,3},{10,4},{11,5},{12,6},{13,7},{14,0},{15,1},{16,8},{17,9... | collective-permute-start | bytes 589832 | tf_op jit(solution)/shard_map/ppermute | solution.py:40
  72.2 14.3 %collective-permute-start.16 = (bf16[64,1536]{1,0:T(8,128)(2,1)S(1)}, bf16[64,1536]{1,0:T(8,128)(2,1)S(1)}, u32[]{:S(2)}, u32[]{:S(2)}) collective-permute-start(bf16[64,1536]{1,0:T(8,128)(2,1)S(1)} %get-tuple-element.42), channel_id=1, source_target_pairs={{8,0},{9,1},{10,2},{11,3},{12,4},{13,5},{14,6},{15,7},{16,14},{17,... | collective-permute-start | bytes 589832 | tf_op jit(solution)/shard_map/ppermute | solution.py:40
  74.1 19.8 %collective-permute-start.20 = (bf16[64,1536]{1,0:T(8,128)(2,1)S(1)}, bf16[64,1536]{1,0:T(8,128)(2,1)S(1)}, u32[]{:S(2)}, u32[]{:S(2)}) collective-permute-start(bf16[64,1536]{1,0:T(8,128)(2,1)S(1)} %get-tuple-element.47), channel_id=1, source_target_pairs={{8,0},{9,1},{10,2},{11,3},{12,4},{13,5},{14,6},{15,7},{16,14},{17,... | collective-permute-start | bytes 589832 | tf_op jit(solution)/shard_map/ppermute | solution.py:40
  78.0 18.0 %collective-permute-start.18 = (bf16[64,1536]{1,0:T(8,128)(2,1)S(1)}, bf16[64,1536]{1,0:T(8,128)(2,1)S(1)}, u32[]{:S(2)}, u32[]{:S(2)}) collective-permute-start(bf16[64,1536]{1,0:T(8,128)(2,1)S(1)} %get-tuple-element.48), channel_id=1, source_target_pairs={{8,2},{9,3},{10,4},{11,5},{12,6},{13,7},{14,0},{15,1},{16,8},{17,9... | collective-permute-start | bytes 589832 | tf_op jit(solution)/shard_map/ppermute | solution.py:40
  81.6 22.9 %collective-permute-start.6 = (bf16[64,1536]{1,0:T(8,128)(2,1)S(1)}, bf16[64,1536]{1,0:T(8,128)(2,1)S(1)}, u32[]{:S(2)}, u32[]{:S(2)}) collective-permute-start(bf16[64,1536]{1,0:T(8,128)(2,1)S(1)} %get-tuple-element.37), channel_id=1, source_target_pairs={{8,2},{9,3},{10,4},{11,5},{12,6},{13,7},{14,0},{15,1},{16,8},{17,9... | collective-permute-start | bytes 589832 | tf_op jit(solution)/shard_map/ppermute | solution.py:40
  84.6 19.9 %collective-permute-start.8 = (bf16[64,1536]{1,0:T(8,128)(2,1)S(1)}, bf16[64,1536]{1,0:T(8,128)(2,1)S(1)}, u32[]{:S(2)}, u32[]{:S(2)}) collective-permute-start(bf16[64,1536]{1,0:T(8,128)(2,1)S(1)} %get-tuple-element.38), channel_id=1, source_target_pairs={{8,0},{9,1},{10,2},{11,3},{12,4},{13,5},{14,6},{15,7},{16,14},{17,... | collective-permute-start | bytes 589832 | tf_op jit(solution)/shard_map/ppermute | solution.py:40
  86.5 23.0 %collective-permute-start.12 = (bf16[64,1536]{1,0:T(8,128)(2,1)S(1)}, bf16[64,1536]{1,0:T(8,128)(2,1)S(1)}, u32[]{:S(2)}, u32[]{:S(2)}) collective-permute-start(bf16[64,1536]{1,0:T(8,128)(2,1)S(1)} %get-tuple-element.45), channel_id=1, source_target_pairs={{8,0},{9,1},{10,2},{11,3},{12,4},{13,5},{14,6},{15,7},{16,14},{17,... | collective-permute-start | bytes 589832 | tf_op jit(solution)/shard_map/ppermute | solution.py:40
  93.9 16.0 %collective-permute-start.10 = (bf16[64,1536]{1,0:T(8,128)(2,1)S(1)}, bf16[64,1536]{1,0:T(8,128)(2,1)S(1)}, u32[]{:S(2)}, u32[]{:S(2)}) collective-permute-start(bf16[64,1536]{1,0:T(8,128)(2,1)S(1)} %get-tuple-element.46), channel_id=1, source_target_pairs={{8,2},{9,3},{10,4},{11,5},{12,6},{13,7},{14,0},{15,1},{16,8},{17,9... | collective-permute-start | bytes 589832 | tf_op jit(solution)/shard_map/ppermute | solution.py:40

commit v3 on v2

--- a/solution.py
+++ b/solution.py
@@ -11,7 +11,7 @@
 TOK = 512
 FEAT = 6144
 AXES = ("section", "tensor")
-GROUPS = ((0, 3), (3, 3))
+GROUPS = ((0, 2), (2, 2), (4, 2))
 PIECES = 4
 TILE = 768
 BLOCK = 128

time: 112 us -> 112 us (level)
  waiting for transfers between devices: 35.9 us -> 33.8 us
  Pallas kernels: 22.7 us -> 24.5 us
    ppermute x21 -> x23, waiting for transfers between devices: 35.9 us -> 33.8 us  [sent(): return lax.ppermute(value, AXES, pairs)]
    pallas_call x2 -> x3, Pallas kernels: 3.24 us -> 4.3 us  [value_gradient(): pl.pallas_call(functools.partial(unpack_kernel, heads), out_shape=(out, o...]
    pallas_call x2 -> x3, Pallas kernels: 6.04 us -> 6.77 us  [packed_probs(): pl.pallas_call(functools.partial(pack_kernel, heads), out_shape=jax.Shape...]
    ppermute x21 -> x23, starting transfers between devices: 46.9 us -> 46.6 us  [sent(): return lax.ppermute(value, AXES, pairs)]
  transfers between devices with their start and end apart: 21 -> 23, of which waited for: 9 -> 10; matrix products, arithmetic and copies ran while one was open for 2% -> 2% of each run, Pallas kernels for 17% -> 19%
where the time goes in v3:
time: 112 us; the launch traced here: 110 us
  starting transfers between devices  46.6 us (42%)
  waiting for transfers between devices  33.8 us (30%)
  Pallas kernels  24.5 us (22%)
  other arithmetic  2.77 us (2%)
  local copies, waits for them, and re-layouts  2.33 us (2%)
    ppermute x23, starting transfers between devices, sent(): return lax.ppermute(value, AXES, pairs)  46.6 us
    ppermute x23, waiting for transfers between devices, sent(): return lax.ppermute(value, AXES, pairs)  33.8 us
    pallas_call x4, Pallas kernels, products(): pl.pallas_call(product_kernel, out_shape=(sent_shape, sent_shape, jax.Sha...  13.4 us
    pallas_call x3, Pallas kernels, packed_probs(): pl.pallas_call(functools.partial(pack_kernel, heads), out_shape=jax.Shape...  6.77 us
    pallas_call x3, Pallas kernels, value_gradient(): pl.pallas_call(functools.partial(unpack_kernel, heads), out_shape=(out, o...  4.3 us
    unnamed x12, local copies, waits for them, and re-layouts  2.3 us
  transfers between devices with their start and end apart: 23, of which 10 were waited for; matrix products, arithmetic and copies ran while one was open for 2% of the time, Pallas kernels for 19%

profile of v3, /device:TPU:46, one launch (start us, length us, event | category | flops | bytes accessed | tf_op | source)
XLA Modules:
  0.0 110.3 jit_solution(15840610024063247502)
XLA Ops:
  2.3 2.3 %shard_map.57 = bf16[272,512]{1,0:T(8,128)(2,1)S(1)} custom-call(s32[4]{0:T(128)S(1)} %pad_add_fusion.place_ref, bf16[1,2,512,768]{3,2,1,0:T(8,128)(2,1)S(1)} %copy-done, s32[32,512]{1,0:T(8,128)S(1)} %copy-done.2), custom_call_target="tpu_custom_call" | custom-call | tf_op jit(solution)/shard_map/pallas_call | solution.py:204
  5.7 2.3 %shard_map.59 = bf16[272,512]{1,0:T(8,128)(2,1)S(1)} custom-call(s32[4]{0:T(128)S(1)} %pad_add_fusion.place_ref, bf16[1,2,512,768]{3,2,1,0:T(8,128)(2,1)S(1)} %copy-done, s32[32,512]{1,0:T(8,128)S(1)} %copy-done.2), custom_call_target="tpu_custom_call" | custom-call | tf_op jit(solution)/shard_map/pallas_call | solution.py:204
  8.0 4.1 %collective-permute-start.2 = (bf16[272,512]{1,0:T(8,128)(2,1)S(1)}, bf16[272,512]{1,0:T(8,128)(2,1)S(1)}, u32[]{:S(2)}, u32[]{:S(2)}) collective-permute-start(bf16[272,512]{1,0:T(8,128)(2,1)S(1)} %shard_map.59), channel_id=1, source_target_pairs={{0,248},{1,249},{2,250},{3,251},{4,252},{5,253},{6,254},{7,255},{8... | collective-permute-start | bytes 835592 | tf_op jit(solution)/shard_map/ppermute | solution.py:40
  12.1 2.3 %shard_map.55 = bf16[272,512]{1,0:T(8,128)(2,1)S(1)} custom-call(s32[4]{0:T(128)S(1)} %pad_add_fusion.place_ref, bf16[1,2,512,768]{3,2,1,0:T(8,128)(2,1)S(1)} %copy-done, s32[32,512]{1,0:T(8,128)S(1)} %copy-done.2), custom_call_target="tpu_custom_call" | custom-call | tf_op jit(solution)/shard_map/pallas_call | solution.py:204
  15.5 1.7 %collective-permute-done.1.packed_ref = bf16[272,512]{1,0:T(8,128)(2,1)S(1)} collective-permute-done((bf16[272,512]{1,0:T(8,128)(2,1)S(1)}, bf16[272,512]{1,0:T(8,128)(2,1)S(1)}, u32[]{:S(2)}, u32[]{:S(2)}) %collective-permute-start.1) | collective-permute-done | bytes 278560 | tf_op jit(solution)/shard_map/ppermute | solution.py:40
  18.7 4.4 %collective-permute-done.2.packed_ref = bf16[272,512]{1,0:T(8,128)(2,1)S(1)} collective-permute-done((bf16[272,512]{1,0:T(8,128)(2,1)S(1)}, bf16[272,512]{1,0:T(8,128)(2,1)S(1)}, u32[]{:S(2)}, u32[]{:S(2)}) %collective-permute-start.2) | collective-permute-done | bytes 278560 | tf_op jit(solution)/shard_map/ppermute | solution.py:40
  23.1 1.4 %shard_map.60 = (bf16[256,256]{1,0:T(8,128)(2,1)S(1)}, bf16[256,256]{1,0:T(8,128)(2,1)S(1)}) custom-call(s32[4]{0:T(128)S(1)} %pad_add_fusion.place_ref, bf16[272,512]{1,0:T(8,128)(2,1)S(1)} %collective-permute-done.2.packed_ref, bf16[1,512,768]{2,1,0:T(8,128)(2,1)S(1)} %copy-done.1, s32[32,512]{1,0:T(8,128)S(1)} %copy-done.2), custom_call_target="tpu_custom_call" | custom-call | tf_op jit(solution)/shard_map/pallas_call | solution.py:227
  24.7 4.0 %collective-permute-done.packed_ref = bf16[272,512]{1,0:T(8,128)(2,1)S(1)} collective-permute-done((bf16[272,512]{1,0:T(8,128)(2,1)S(1)}, bf16[272,512]{1,0:T(8,128)(2,1)S(1)}, u32[]{:S(2)}, u32[]{:S(2)}) %collective-permute-start) | collective-permute-done | bytes 278560 | tf_op jit(solution)/shard_map/ppermute | solution.py:40
  28.7 1.4 %shard_map.56 = (bf16[256,256]{1,0:T(8,128)(2,1)S(1)}, bf16[256,256]{1,0:T(8,128)(2,1)S(1)}) custom-call(s32[4]{0:T(128)S(1)} %pad_add_fusion.place_ref, bf16[272,512]{1,0:T(8,128)(2,1)S(1)} %collective-permute-done.packed_ref, bf16[1,512,768]{2,1,0:T(8,128)(2,1)S(1)} %copy-done.1, s32[32,512]{1,0:T(8,128)S(1)} %copy-done.2), custom_call_target="tpu_custom_call" | custom-call | tf_op jit(solution)/shard_map/pallas_call | solution.py:227
  31.7 3.4 %shard_map.64 = (bf16[64,1536]{1,0:T(8,128)(2,1)S(1)}, bf16[64,1536]{1,0:T(8,128)(2,1)S(1)}, f32[128,1536]{1,0:T(8,128)S(1)}) custom-call(bf16[256,768]{1,0:T(8,128)(2,1)S(1)} %constant_dynamic-update-slice_fusion.own_ref, bf16[256,768]{1,0:T(8,128)(2,1)S(1)} %constant_dynamic-update-slice_fusion.3.taken_ref, bf16[1,6144,768]{2,1,0:T(8,128)(2,1)} %weight_ref.7, ...), custom_call_target="tpu_custom_call" | custom-call | tf_op jit(solution)/shard_map/pallas_call | solution.py:259
  35.1 3.3 %collective-permute-start.19 = (bf16[64,1536]{1,0:T(8,128)(2,1)S(1)}, bf16[64,1536]{1,0:T(8,128)(2,1)S(1)}, u32[]{:S(2)}, u32[]{:S(2)}) collective-permute-start(bf16[64,1536]{1,0:T(8,128)(2,1)S(1)} %get-tuple-element.39), channel_id=1, source_target_pairs={{0,2},{1,3},{2,4},{3,5},{4,6},{5,7},{6,0},{7,1},{8,10},{9,11},{10,... | collective-permute-start | bytes 589832 | tf_op jit(solution)/shard_map/ppermute | solution.py:40
  38.4 2.4 %collective-permute-start.21 = (bf16[64,1536]{1,0:T(8,128)(2,1)S(1)}, bf16[64,1536]{1,0:T(8,128)(2,1)S(1)}, u32[]{:S(2)}, u32[]{:S(2)}) collective-permute-start(bf16[64,1536]{1,0:T(8,128)(2,1)S(1)} %get-tuple-element.40), channel_id=1, source_target_pairs={{0,6},{1,7},{2,0},{3,1},{4,2},{5,3},{6,4},{7,5},{8,14},{9,15},{10,... | collective-permute-start | bytes 589832 | tf_op jit(solution)/shard_map/ppermute | solution.py:40
  40.8 3.4 %shard_map.63 = (bf16[64,1536]{1,0:T(8,128)(2,1)S(1)}, bf16[64,1536]{1,0:T(8,128)(2,1)S(1)}, f32[128,1536]{1,0:T(8,128)S(1)}) custom-call(bf16[256,768]{1,0:T(8,128)(2,1)S(1)} %constant_dynamic-update-slice_fusion.own_ref, bf16[256,768]{1,0:T(8,128)(2,1)S(1)} %constant_dynamic-update-slice_fusion.3.taken_ref, bf16[1,6144,768]{2,1,0:T(8,128)(2,1)} %weight_ref.7, ...), custom_call_target="tpu_custom_call" | custom-call | tf_op jit(solution)/shard_map/pallas_call | solution.py:259
  45.4 2.9 %collective-permute-start.17 = (bf16[64,1536]{1,0:T(8,128)(2,1)S(1)}, bf16[64,1536]{1,0:T(8,128)(2,1)}, u32[]{:S(2)}, u32[]{:S(2)}) collective-permute-start(bf16[64,1536]{1,0:T(8,128)(2,1)S(1)} %get-tuple-element.37), channel_id=1, source_target_pairs={{0,6},{1,7},{2,0},{3,1},{4,2},{5,3},{6,4},{7,5},{8,14},{9,15},{10,... | collective-permute-start | bytes 589832 | tf_op jit(solution)/shard_map/ppermute | solution.py:40
  48.4 3.4 %shard_map.62 = (bf16[64,1536]{1,0:T(8,128)(2,1)S(1)}, bf16[64,1536]{1,0:T(8,128)(2,1)S(1)}, f32[128,1536]{1,0:T(8,128)S(1)}) custom-call(bf16[256,768]{1,0:T(8,128)(2,1)S(1)} %constant_dynamic-update-slice_fusion.own_ref, bf16[256,768]{1,0:T(8,128)(2,1)S(1)} %constant_dynamic-update-slice_fusion.3.taken_ref, bf16[1,6144,768]{2,1,0:T(8,128)(2,1)} %weight_ref.7, ...), custom_call_target="tpu_custom_call" | custom-call | tf_op jit(solution)/shard_map/pallas_call | solution.py:259
  53.0 3.4 %shard_map.61 = (bf16[64,1536]{1,0:T(8,128)(2,1)S(1)}, bf16[64,1536]{1,0:T(8,128)(2,1)S(1)}, f32[128,1536]{1,0:T(8,128)S(1)}) custom-call(bf16[256,768]{1,0:T(8,128)(2,1)S(1)} %constant_dynamic-update-slice_fusion.own_ref, bf16[256,768]{1,0:T(8,128)(2,1)S(1)} %constant_dynamic-update-slice_fusion.3.taken_ref, bf16[1,6144,768]{2,1,0:T(8,128)(2,1)} %weight_ref.7, ...), custom_call_target="tpu_custom_call" | custom-call | tf_op jit(solution)/shard_map/pallas_call | solution.py:259
  56.4 3.0 %collective-permute-start.13 = (bf16[64,1536]{1,0:T(8,128)(2,1)S(1)}, bf16[64,1536]{1,0:T(8,128)(2,1)S(1)}, u32[]{:S(2)}, u32[]{:S(2)}) collective-permute-start(bf16[64,1536]{1,0:T(8,128)(2,1)S(1)} %get-tuple-element.34), channel_id=1, source_target_pairs={{0,6},{1,7},{2,0},{3,1},{4,2},{5,3},{6,4},{7,5},{8,14},{9,15},{10,... | collective-permute-start | bytes 589832 | tf_op jit(solution)/shard_map/ppermute | solution.py:40
  60.7 2.9 %collective-permute-start.9 = (bf16[64,1536]{1,0:T(8,128)(2,1)S(1)}, bf16[64,1536]{1,0:T(8,128)(2,1)S(1)}, u32[]{:S(2)}, u32[]{:S(2)}) collective-permute-start(bf16[64,1536]{1,0:T(8,128)(2,1)S(1)} %get-tuple-element.31), channel_id=1, source_target_pairs={{0,6},{1,7},{2,0},{3,1},{4,2},{5,3},{6,4},{7,5},{8,14},{9,15},{10,... | collective-permute-start | bytes 589832 | tf_op jit(solution)/shard_map/ppermute | solution.py:40
  64.9 2.7 %collective-permute-start.16 = (bf16[64,1536]{1,0:T(8,128)(2,1)S(1)}, bf16[64,1536]{1,0:T(8,128)(2,1)S(1)}, u32[]{:S(2)}, u32[]{:S(2)}) collective-permute-start(bf16[64,1536]{1,0:T(8,128)(2,1)S(1)} %get-tuple-element.45), channel_id=1, source_target_pairs={{8,2},{9,3},{10,4},{11,5},{12,6},{13,7},{14,0},{15,1},{16,8},{17,9... | collective-permute-start | bytes 589832 | tf_op jit(solution)/shard_map/ppermute | solution.py:40
  67.5 3.9 %collective-permute-done.11 = bf16[64,1536]{1,0:T(8,128)(2,1)S(1)} collective-permute-done((bf16[64,1536]{1,0:T(8,128)(2,1)S(1)}, bf16[64,1536]{1,0:T(8,128)(2,1)S(1)}, u32[]{:S(2)}, u32[]{:S(2)}) %collective-permute-start.11) | collective-permute-done | bytes 196640 | tf_op jit(solution)/shard_map/ppermute | solution.py:40
  71.4 1.9 %collective-permute-start.18 = (bf16[64,1536]{1,0:T(8,128)(2,1)S(1)}, bf16[64,1536]{1,0:T(8,128)(2,1)S(1)}, u32[]{:S(2)}, u32[]{:S(2)}) collective-permute-start(bf16[64,1536]{1,0:T(8,128)(2,1)S(1)} %get-tuple-element.46), channel_id=1, source_target_pairs={{8,0},{9,1},{10,2},{11,3},{12,4},{13,5},{14,6},{15,7},{16,14},{17,... | collective-permute-start | bytes 589832 | tf_op jit(solution)/shard_map/ppermute | solution.py:40
  73.3 3.8 %collective-permute-start.22 = (bf16[64,1536]{1,0:T(8,128)(2,1)S(1)}, bf16[64,1536]{1,0:T(8,128)(2,1)S(1)}, u32[]{:S(2)}, u32[]{:S(2)}) collective-permute-start(bf16[64,1536]{1,0:T(8,128)(2,1)S(1)} %get-tuple-element.51), channel_id=1, source_target_pairs={{8,0},{9,1},{10,2},{11,3},{12,4},{13,5},{14,6},{15,7},{16,14},{17,... | collective-permute-start | bytes 589832 | tf_op jit(solution)/shard_map/ppermute | solution.py:40
  77.2 3.2 %collective-permute-start.20 = (bf16[64,1536]{1,0:T(8,128)(2,1)S(1)}, bf16[64,1536]{1,0:T(8,128)(2,1)S(1)}, u32[]{:S(2)}, u32[]{:S(2)}) collective-permute-start(bf16[64,1536]{1,0:T(8,128)(2,1)S(1)} %get-tuple-element.52), channel_id=1, source_target_pairs={{8,2},{9,3},{10,4},{11,5},{12,6},{13,7},{14,0},{15,1},{16,8},{17,9... | collective-permute-start | bytes 589832 | tf_op jit(solution)/shard_map/ppermute | solution.py:40
  80.7 3.1 %collective-permute-start.8 = (bf16[64,1536]{1,0:T(8,128)(2,1)S(1)}, bf16[64,1536]{1,0:T(8,128)(2,1)S(1)}, u32[]{:S(2)}, u32[]{:S(2)}) collective-permute-start(bf16[64,1536]{1,0:T(8,128)(2,1)S(1)} %get-tuple-element.41), channel_id=1, source_target_pairs={{8,2},{9,3},{10,4},{11,5},{12,6},{13,7},{14,0},{15,1},{16,8},{17,9... | collective-permute-start | bytes 589832 | tf_op jit(solution)/shard_map/ppermute | solution.py:40
  83.7 1.9 %collective-permute-start.10 = (bf16[64,1536]{1,0:T(8,128)(2,1)S(1)}, bf16[64,1536]{1,0:T(8,128)(2,1)S(1)}, u32[]{:S(2)}, u32[]{:S(2)}) collective-permute-start(bf16[64,1536]{1,0:T(8,128)(2,1)S(1)} %get-tuple-element.42), channel_id=1, source_target_pairs={{8,0},{9,1},{10,2},{11,3},{12,4},{13,5},{14,6},{15,7},{16,14},{17,... | collective-permute-start | bytes 589832 | tf_op jit(solution)/shard_map/ppermute | solution.py:40
  85.7 1.6 %collective-permute-done.18 = bf16[64,1536]{1,0:T(8,128)(2,1)S(1)} collective-permute-done((bf16[64,1536]{1,0:T(8,128)(2,1)S(1)}, bf16[64,1536]{1,0:T(8,128)(2,1)S(1)}, u32[]{:S(2)}, u32[]{:S(2)}) %collective-permute-start.18) | collective-permute-done | bytes 196640 | tf_op jit(solution)/shard_map/ppermute | solution.py:40
  87.3 3.1 %collective-permute-start.14 = (bf16[64,1536]{1,0:T(8,128)(2,1)S(1)}, bf16[64,1536]{1,0:T(8,128)(2,1)S(1)}, u32[]{:S(2)}, u32[]{:S(2)}) collective-permute-start(bf16[64,1536]{1,0:T(8,128)(2,1)S(1)} %get-tuple-element.49), channel_id=1, source_target_pairs={{8,0},{9,1},{10,2},{11,3},{12,4},{13,5},{14,6},{15,7},{16,14},{17,... | collective-permute-start | bytes 589832 | tf_op jit(solution)/shard_map/ppermute | solution.py:40
  90.5 4.7 %collective-permute-done.22 = bf16[64,1536]{1,0:T(8,128)(2,1)S(1)} collective-permute-done((bf16[64,1536]{1,0:T(8,128)(2,1)S(1)}, bf16[64,1536]{1,0:T(8,128)(2,1)S(1)}, u32[]{:S(2)}, u32[]{:S(2)}) %collective-permute-start.22) | collective-permute-done | bytes 196640 | tf_op jit(solution)/shard_map/ppermute | solution.py:40
  95.2 1.9 %collective-permute-start.12 = (bf16[64,1536]{1,0:T(8,128)(2,1)S(1)}, bf16[64,1536]{1,0:T(8,128)(2,1)S(1)}, u32[]{:S(2)}, u32[]{:S(2)}) collective-permute-start(bf16[64,1536]{1,0:T(8,128)(2,1)S(1)} %get-tuple-element.50), channel_id=1, source_target_pairs={{8,2},{9,3},{10,4},{11,5},{12,6},{13,7},{14,0},{15,1},{16,8},{17,9... | collective-permute-start | bytes 589832 | tf_op jit(solution)/shard_map/ppermute | solution.py:40
  97.2 4.9 %collective-permute-done.8 = bf16[64,1536]{1,0:T(8,128)(2,1)S(1)} collective-permute-done((bf16[64,1536]{1,0:T(8,128)(2,1)S(1)}, bf16[64,1536]{1,0:T(8,128)(2,1)S(1)}, u32[]{:S(2)}, u32[]{:S(2)}) %collective-permute-start.8) | collective-permute-done | bytes 196640 | tf_op jit(solution)/shard_map/ppermute | solution.py:40
  102.1 1.6 %collective-permute-done.10 = bf16[64,1536]{1,0:T(8,128)(2,1)S(1)} collective-permute-done((bf16[64,1536]{1,0:T(8,128)(2,1)S(1)}, bf16[64,1536]{1,0:T(8,128)(2,1)S(1)}, u32[]{:S(2)}, u32[]{:S(2)}) %collective-permute-start.10) | collective-permute-done | bytes 196640 | tf_op jit(solution)/shard_map/ppermute | solution.py:40
  103.7 5.6 %collective-permute-done.14 = bf16[64,1536]{1,0:T(8,128)(2,1)S(1)} collective-permute-done((bf16[64,1536]{1,0:T(8,128)(2,1)S(1)}, bf16[64,1536]{1,0:T(8,128)(2,1)S(1)}, u32[]{:S(2)}, u32[]{:S(2)}) %collective-permute-start.14) | collective-permute-done | bytes 196640 | tf_op jit(solution)/shard_map/ppermute | solution.py:40
  (46 shorter events, 14.2 us)
Async XLA Ops:
  0.0 31.7 %collective-permute-start.6 = (bf16[6144,768]{1,0:T(8,128)(2,1)}, bf16[6144,768]{1,0:T(8,128)(2,1)}, u32[]{:S(2)}, u32[]{:S(2)}) collective-permute-start(bf16[6144,768]{1,0:T(8,128)(2,1)} %bitcast.8), channel_id=1, source_target_pairs={{0,1},{1,0},{2,3},{3,2},{4,5},{5,4},{6,7},{7,6},{8,9},{9,8},{10,11... | collective-permute-start | bytes 28311560 | tf_op jit(solution)/shard_map/ppermute | solution.py:40
  0.1 1.4 %copy-start = (bf16[1,2,512,768]{3,2,1,0:T(8,128)(2,1)S(1)}, bf16[1,2,512,768]{3,2,1,0:T(8,128)(2,1)}, u32[]{:S(2)}) copy-start(bf16[1,2,512,768]{3,2,1,0:T(8,128)(2,1)} %stash_ref.5) | copy-start | bytes 4718596
  1.5 0.8 copy-start.2
  4.6 12.6 %copy-start.1 = (bf16[1,512,768]{2,1,0:T(8,128)(2,1)S(1)}, bf16[1,512,768]{2,1,0:T(8,128)(2,1)}, u32[]{:S(2)}) copy-start(bf16[1,512,768]{2,1,0:T(8,128)(2,1)} %grad_ref.5) | copy-start | bytes 2359300
  4.6 12.5 %collective-permute-start.1 = (bf16[272,512]{1,0:T(8,128)(2,1)S(1)}, bf16[272,512]{1,0:T(8,128)(2,1)S(1)}, u32[]{:S(2)}, u32[]{:S(2)}) collective-permute-start(bf16[272,512]{1,0:T(8,128)(2,1)S(1)} %shard_map.57), channel_id=1, source_target_pairs={{0,248},{1,249},{2,250},{3,251},{4,252},{5,253},{6,254},{7,255},{8... | collective-permute-start | bytes 835592 | tf_op jit(solution)/shard_map/ppermute | solution.py:40
  8.0 15.1 %collective-permute-start.2 = (bf16[272,512]{1,0:T(8,128)(2,1)S(1)}, bf16[272,512]{1,0:T(8,128)(2,1)S(1)}, u32[]{:S(2)}, u32[]{:S(2)}) collective-permute-start(bf16[272,512]{1,0:T(8,128)(2,1)S(1)} %shard_map.59), channel_id=1, source_target_pairs={{0,248},{1,249},{2,250},{3,251},{4,252},{5,253},{6,254},{7,255},{8... | collective-permute-start | bytes 835592 | tf_op jit(solution)/shard_map/ppermute | solution.py:40
  14.3 14.4 %collective-permute-start = (bf16[272,512]{1,0:T(8,128)(2,1)S(1)}, bf16[272,512]{1,0:T(8,128)(2,1)S(1)}, u32[]{:S(2)}, u32[]{:S(2)}) collective-permute-start(bf16[272,512]{1,0:T(8,128)(2,1)S(1)} %shard_map.55), channel_id=1, source_target_pairs={{0,248},{1,249},{2,250},{3,251},{4,252},{5,253},{6,254},{7,255},{8... | collective-permute-start | bytes 835592 | tf_op jit(solution)/shard_map/ppermute | solution.py:40
  18.6 13.0 %collective-permute-start.4 = (bf16[256,256]{1,0:T(8,128)(2,1)S(1)}, bf16[256,256]{1,0:T(8,128)(2,1)S(1)}, u32[]{:S(2)}, u32[]{:S(2)}) collective-permute-start(bf16[256,256]{1,0:T(8,128)(2,1)S(1)} %get-tuple-element.27), channel_id=1, source_target_pairs={{0,1},{1,0},{2,3},{3,2},{4,5},{5,4},{6,7},{7,6},{8,9},{9,8},{10,11... | collective-permute-start | bytes 393224 | tf_op jit(solution)/shard_map/ppermute | solution.py:40
  24.6 7.1 %collective-permute-start.5 = (bf16[256,256]{1,0:T(8,128)(2,1)S(1)}, bf16[256,256]{1,0:T(8,128)(2,1)S(1)}, u32[]{:S(2)}, u32[]{:S(2)}) collective-permute-start(bf16[256,256]{1,0:T(8,128)(2,1)S(1)} %get-tuple-element.28), channel_id=1, source_target_pairs={{0,1},{1,0},{2,3},{3,2},{4,5},{5,4},{6,7},{7,6},{8,9},{9,8},{10,11... | collective-permute-start | bytes 393224 | tf_op jit(solution)/shard_map/ppermute | solution.py:40
  30.2 1.4 %collective-permute-start.3 = (bf16[256,256]{1,0:T(8,128)(2,1)S(1)}, bf16[256,256]{1,0:T(8,128)(2,1)S(1)}, u32[]{:S(2)}, u32[]{:S(2)}) collective-permute-start(bf16[256,256]{1,0:T(8,128)(2,1)S(1)} %get-tuple-element.26), channel_id=1, source_target_pairs={{0,1},{1,0},{2,3},{3,2},{4,5},{5,4},{6,7},{7,6},{8,9},{9,8},{10,11... | collective-permute-start | bytes 393224 | tf_op jit(solution)/shard_map/ppermute | solution.py:40
  35.1 21.3 %collective-permute-start.19 = (bf16[64,1536]{1,0:T(8,128)(2,1)S(1)}, bf16[64,1536]{1,0:T(8,128)(2,1)S(1)}, u32[]{:S(2)}, u32[]{:S(2)}) collective-permute-start(bf16[64,1536]{1,0:T(8,128)(2,1)S(1)} %get-tuple-element.39), channel_id=1, source_target_pairs={{0,2},{1,3},{2,4},{3,5},{4,6},{5,7},{6,0},{7,1},{8,10},{9,11},{10,... | collective-permute-start | bytes 589832 | tf_op jit(solution)/shard_map/ppermute | solution.py:40
  38.4 21.0 %collective-permute-start.21 = (bf16[64,1536]{1,0:T(8,128)(2,1)S(1)}, bf16[64,1536]{1,0:T(8,128)(2,1)S(1)}, u32[]{:S(2)}, u32[]{:S(2)}) collective-permute-start(bf16[64,1536]{1,0:T(8,128)(2,1)S(1)} %get-tuple-element.40), channel_id=1, source_target_pairs={{0,6},{1,7},{2,0},{3,1},{4,2},{5,3},{6,4},{7,5},{8,14},{9,15},{10,... | collective-permute-start | bytes 589832 | tf_op jit(solution)/shard_map/ppermute | solution.py:40
  44.2 16.5 %collective-permute-start.15 = (bf16[64,1536]{1,0:T(8,128)(2,1)S(1)}, bf16[64,1536]{1,0:T(8,128)(2,1)}, u32[]{:S(2)}, u32[]{:S(2)}) collective-permute-start(bf16[64,1536]{1,0:T(8,128)(2,1)S(1)} %get-tuple-element.36), channel_id=1, source_target_pairs={{0,2},{1,3},{2,4},{3,5},{4,6},{5,7},{6,0},{7,1},{8,10},{9,11},{10,... | collective-permute-start | bytes 589832 | tf_op jit(solution)/shard_map/ppermute | solution.py:40
  45.4 18.1 %collective-permute-start.17 = (bf16[64,1536]{1,0:T(8,128)(2,1)S(1)}, bf16[64,1536]{1,0:T(8,128)(2,1)}, u32[]{:S(2)}, u32[]{:S(2)}) collective-permute-start(bf16[64,1536]{1,0:T(8,128)(2,1)S(1)} %get-tuple-element.37), channel_id=1, source_target_pairs={{0,6},{1,7},{2,0},{3,1},{4,2},{5,3},{6,4},{7,5},{8,14},{9,15},{10,... | collective-permute-start | bytes 589832 | tf_op jit(solution)/shard_map/ppermute | solution.py:40
  51.8 11.8 %copy-start.3 = (bf16[1,64,6144]{2,1,0:T(8,128)(2,1)S(1)}, bf16[1,64,6144]{2,1,0:T(8,128)(2,1)}, u32[]{:S(2)}) copy-start(bf16[1,64,6144]{2,1,0:T(8,128)(2,1)} %param.9) | copy-start | bytes 2359300
  51.8 19.6 %collective-permute-start.11 = (bf16[64,1536]{1,0:T(8,128)(2,1)S(1)}, bf16[64,1536]{1,0:T(8,128)(2,1)S(1)}, u32[]{:S(2)}, u32[]{:S(2)}) collective-permute-start(bf16[64,1536]{1,0:T(8,128)(2,1)S(1)} %get-tuple-element.33), channel_id=1, source_target_pairs={{0,2},{1,3},{2,4},{3,5},{4,6},{5,7},{6,0},{7,1},{8,10},{9,11},{10,... | collective-permute-start | bytes 589832 | tf_op jit(solution)/shard_map/ppermute | solution.py:40
  56.4 16.9 %collective-permute-start.13 = (bf16[64,1536]{1,0:T(8,128)(2,1)S(1)}, bf16[64,1536]{1,0:T(8,128)(2,1)S(1)}, u32[]{:S(2)}, u32[]{:S(2)}) collective-permute-start(bf16[64,1536]{1,0:T(8,128)(2,1)S(1)} %get-tuple-element.34), channel_id=1, source_target_pairs={{0,6},{1,7},{2,0},{3,1},{4,2},{5,3},{6,4},{7,5},{8,14},{9,15},{10,... | collective-permute-start | bytes 589832 | tf_op jit(solution)/shard_map/ppermute | solution.py:40
  59.4 17.8 %collective-permute-start.7 = (bf16[64,1536]{1,0:T(8,128)(2,1)S(1)}, bf16[64,1536]{1,0:T(8,128)(2,1)S(1)}, u32[]{:S(2)}, u32[]{:S(2)}) collective-permute-start(bf16[64,1536]{1,0:T(8,128)(2,1)S(1)} %get-tuple-element.30), channel_id=1, source_target_pairs={{0,2},{1,3},{2,4},{3,5},{4,6},{5,7},{6,0},{7,1},{8,10},{9,11},{10,... | collective-permute-start | bytes 589832 | tf_op jit(solution)/shard_map/ppermute | solution.py:40
  60.7 19.7 %collective-permute-start.9 = (bf16[64,1536]{1,0:T(8,128)(2,1)S(1)}, bf16[64,1536]{1,0:T(8,128)(2,1)S(1)}, u32[]{:S(2)}, u32[]{:S(2)}) collective-permute-start(bf16[64,1536]{1,0:T(8,128)(2,1)S(1)} %get-tuple-element.31), channel_id=1, source_target_pairs={{0,6},{1,7},{2,0},{3,1},{4,2},{5,3},{6,4},{7,5},{8,14},{9,15},{10,... | collective-permute-start | bytes 589832 | tf_op jit(solution)/shard_map/ppermute | solution.py:40
  64.9 18.9 %collective-permute-start.16 = (bf16[64,1536]{1,0:T(8,128)(2,1)S(1)}, bf16[64,1536]{1,0:T(8,128)(2,1)S(1)}, u32[]{:S(2)}, u32[]{:S(2)}) collective-permute-start(bf16[64,1536]{1,0:T(8,128)(2,1)S(1)} %get-tuple-element.45), channel_id=1, source_target_pairs={{8,2},{9,3},{10,4},{11,5},{12,6},{13,7},{14,0},{15,1},{16,8},{17,9... | collective-permute-start | bytes 589832 | tf_op jit(solution)/shard_map/ppermute | solution.py:40
  71.4 15.9 %collective-permute-start.18 = (bf16[64,1536]{1,0:T(8,128)(2,1)S(1)}, bf16[64,1536]{1,0:T(8,128)(2,1)S(1)}, u32[]{:S(2)}, u32[]{:S(2)}) collective-permute-start(bf16[64,1536]{1,0:T(8,128)(2,1)S(1)} %get-tuple-element.46), channel_id=1, source_target_pairs={{8,0},{9,1},{10,2},{11,3},{12,4},{13,5},{14,6},{15,7},{16,14},{17,... | collective-permute-start | bytes 589832 | tf_op jit(solution)/shard_map/ppermute | solution.py:40
  73.3 21.9 %collective-permute-start.22 = (bf16[64,1536]{1,0:T(8,128)(2,1)S(1)}, bf16[64,1536]{1,0:T(8,128)(2,1)S(1)}, u32[]{:S(2)}, u32[]{:S(2)}) collective-permute-start(bf16[64,1536]{1,0:T(8,128)(2,1)S(1)} %get-tuple-element.51), channel_id=1, source_target_pairs={{8,0},{9,1},{10,2},{11,3},{12,4},{13,5},{14,6},{15,7},{16,14},{17,... | collective-permute-start | bytes 589832 | tf_op jit(solution)/shard_map/ppermute | solution.py:40
  77.2 19.9 %collective-permute-start.20 = (bf16[64,1536]{1,0:T(8,128)(2,1)S(1)}, bf16[64,1536]{1,0:T(8,128)(2,1)S(1)}, u32[]{:S(2)}, u32[]{:S(2)}) collective-permute-start(bf16[64,1536]{1,0:T(8,128)(2,1)S(1)} %get-tuple-element.52), channel_id=1, source_target_pairs={{8,2},{9,3},{10,4},{11,5},{12,6},{13,7},{14,0},{15,1},{16,8},{17,9... | collective-permute-start | bytes 589832 | tf_op jit(solution)/shard_map/ppermute | solution.py:40
  80.7 21.4 %collective-permute-start.8 = (bf16[64,1536]{1,0:T(8,128)(2,1)S(1)}, bf16[64,1536]{1,0:T(8,128)(2,1)S(1)}, u32[]{:S(2)}, u32[]{:S(2)}) collective-permute-start(bf16[64,1536]{1,0:T(8,128)(2,1)S(1)} %get-tuple-element.41), channel_id=1, source_target_pairs={{8,2},{9,3},{10,4},{11,5},{12,6},{13,7},{14,0},{15,1},{16,8},{17,9... | collective-permute-start | bytes 589832 | tf_op jit(solution)/shard_map/ppermute | solution.py:40
  83.7 19.9 %collective-permute-start.10 = (bf16[64,1536]{1,0:T(8,128)(2,1)S(1)}, bf16[64,1536]{1,0:T(8,128)(2,1)S(1)}, u32[]{:S(2)}, u32[]{:S(2)}) collective-permute-start(bf16[64,1536]{1,0:T(8,128)(2,1)S(1)} %get-tuple-element.42), channel_id=1, source_target_pairs={{8,0},{9,1},{10,2},{11,3},{12,4},{13,5},{14,6},{15,7},{16,14},{17,... | collective-permute-start | bytes 589832 | tf_op jit(solution)/shard_map/ppermute | solution.py:40
  87.3 22.0 %collective-permute-start.14 = (bf16[64,1536]{1,0:T(8,128)(2,1)S(1)}, bf16[64,1536]{1,0:T(8,128)(2,1)S(1)}, u32[]{:S(2)}, u32[]{:S(2)}) collective-permute-start(bf16[64,1536]{1,0:T(8,128)(2,1)S(1)} %get-tuple-element.49), channel_id=1, source_target_pairs={{8,0},{9,1},{10,2},{11,3},{12,4},{13,5},{14,6},{15,7},{16,14},{17,... | collective-permute-start | bytes 589832 | tf_op jit(solution)/shard_map/ppermute | solution.py:40
  95.2 14.1 %collective-permute-start.12 = (bf16[64,1536]{1,0:T(8,128)(2,1)S(1)}, bf16[64,1536]{1,0:T(8,128)(2,1)S(1)}, u32[]{:S(2)}, u32[]{:S(2)}) collective-permute-start(bf16[64,1536]{1,0:T(8,128)(2,1)S(1)} %get-tuple-element.50), channel_id=1, source_target_pairs={{8,2},{9,3},{10,4},{11,5},{12,6},{13,7},{14,0},{15,1},{16,8},{17,9... | collective-permute-start | bytes 589832 | tf_op jit(solution)/shard_map/ppermute | solution.py:40
